TPU v7x, 512 devices: a whole 4x8x8 slice. The times are simulated.
512 devices in a mesh: ctx: 64 (over z, x, core), head: 8 (over y).
Axes of the slice: x: 4, y: 8, z: 8, core: 2. Of those that a mesh axis runs over, the one named last changes fastest.
Arguments:
- hidden: bfloat16 [2, 4, 16384], P(None, None, 'ctx'), may hold values from -400 to 400
- norm_gain: bfloat16 [16384], P('ctx'), may hold values from 0.099609375 to 1.8984375
- w_query: bfloat16 [16384, 16384], P('ctx', 'head'), may hold values from -0.046875 to 0.046875
- w_keyval: bfloat16 [16384, 2048], P('ctx', 'head'), may hold values from -0.046875 to 0.046875
- w_out: bfloat16 [16384, 16384], P('head', 'ctx'), may hold values from -6 to 6
- cache: bfloat16 [2048, 128, 8, 256], P('ctx', None, 'head'), may hold values from -240 to 240
- page_table: int32 [4, 256], replicated, may hold values from -1 to 2047, as said below
- lengths: int32 [4], replicated, may hold values from 16384 to 32768, as said below
- owners: int32 [4], replicated, may hold values from 0 to 63, as said below
Outputs:
- delivered: bfloat16 [64, 2, 16384], P('ctx')
Inputs may be any that keep to these rules, and one draw needn't show every extreme that they name: `page_table`: entries of one table are distinct page numbers or -1; entry k of request b is a page number exactly when k < ceil(lengths[b] / 128). One index of ctx holds up to 32 used pages, and the used pages lie unevenly over ctx. `lengths`: some request has exactly 32768 cached tokens. `owners`: distinct slots.
All inputs are finite; a program needn't handle non-finite values.
Results may differ from a plain program's by a relative error of at most 0.022.
The roundings to bfloat16 on the way count: a program that leaves them out, or rounds other values in their place, can miss the bound.
Values may be sent and summed in bfloat16 or wider, within the bound.
No kernel may reach another device: no remote copies, remote signals or barrier semaphores. Data moves between devices by JAX's collectives and lax.ppermute only.
A program may use at most 64 MiB of HBM per device.

v0:
```python
import math

import jax
import jax.numpy as jnp
from jax import lax
from jax.sharding import PartitionSpec as P

HD = 128


epsilon = 1e-05
NEGATIVE = -1e30


def frequencies(head_size):
    halfway = head_size // 2
    inverse = 500000.0 ** (-(jnp.arange(halfway, dtype=jnp.float32) * 2.0 / head_size))
    wavelength = 2.0 * math.pi / inverse
    smooth = (8192.0 / wavelength - 1.0) / 3.0
    blended = (1.0 - smooth) * inverse / 8.0 + smooth * inverse
    return jnp.where(
        wavelength < 2048.0, inverse, jnp.where(wavelength > 8192.0, inverse / 8.0, blended)
    )


def rotate(vector, position):
    halfway = vector.shape[-1] // 2
    inverse = frequencies(vector.shape[-1])
    angles = position[..., None] * inverse
    angles = jnp.concatenate([angles, angles], axis=-1)
    turned = jnp.concatenate([-vector[..., halfway:], vector[..., :halfway]], axis=-1)
    return vector * jnp.cos(angles) + turned * jnp.sin(angles)


def body(hidden, norm_gain, w_query, w_keyval, w_out, cache, page_table, lengths, owners):
    n_steps, n_reqs, width_local = hidden.shape
    width_total = width_local * lax.axis_size("ctx")
    hidden_f = hidden.astype(jnp.float32)
    squares = lax.psum(jnp.sum(hidden_f * hidden_f, axis=-1), "ctx")
    normed = (
        hidden_f
        * norm_gain.astype(jnp.float32)
        * lax.rsqrt(squares / width_total + epsilon)[..., None]
    ).astype(jnp.bfloat16)
    flattened = normed.reshape(n_steps * n_reqs, width_local)
    query_part = jnp.dot(flattened, w_query, preferred_element_type=jnp.float32)
    keyval_part = jnp.dot(flattened, w_keyval, preferred_element_type=jnp.float32)
    kv_local = w_keyval.shape[1] // (2 * HD)
    group_size = w_query.shape[1] // (HD * kv_local)
    position = (lengths[None, :] + jnp.arange(n_steps, dtype=jnp.int32)[:, None]).astype(
        jnp.float32
    )
    query_sum, keyval_sum = lax.psum((query_part, keyval_part), "ctx")
    query_raw = query_sum.reshape(n_steps, n_reqs, kv_local, group_size, HD)
    keyval_raw = keyval_sum.reshape(n_steps, n_reqs, kv_local, 2 * HD)
    queries = rotate(query_raw, position[:, :, None, None]).astype(jnp.bfloat16)
    new_keys = rotate(keyval_raw[..., :HD], position[:, :, None]).astype(jnp.bfloat16)
    new_values = keyval_raw[..., HD:].astype(jnp.bfloat16)
    softmax_scale = HD ** (-0.5)
    slots_local, page_len = (cache.shape[0], cache.shape[1])
    tokens = cache.reshape(slots_local * page_len, kv_local, 2 * HD)
    keys_local = tokens[..., :HD]
    values_local = tokens[..., HD:]
    device_now = lax.axis_index("ctx")
    global_ids = device_now * slots_local + jnp.arange(slots_local, dtype=jnp.int32)
    matches = page_table[:, :, None] == global_ids[None, None, :]
    logical = jnp.sum(
        jnp.where(matches, jnp.arange(page_table.shape[1], dtype=jnp.int32)[None, :, None], 0),
        axis=1,
    )
    held = jnp.any(matches, axis=1)
    token_pos = (
        logical[:, :, None] * page_len + jnp.arange(page_len, dtype=jnp.int32)[None, None, :]
    )
    valid = (held[:, :, None] & (token_pos < lengths[:, None, None])).reshape(
        n_reqs, slots_local * page_len
    )
    scores = (
        jnp.einsum("sbkgd,tkd->bskgt", queries, keys_local, preferred_element_type=jnp.float32)
        * softmax_scale
    )
    scores = jnp.where(valid[:, None, None, None, :], scores, NEGATIVE)
    owned = owners == device_now
    causal = jnp.arange(n_steps)[None, :] <= jnp.arange(n_steps)[:, None]
    new_valid = owned[:, None, None, None, None] & causal[None, :, None, None, :]
    new_scores = (
        jnp.einsum("sbkgd,tbkd->bskgt", queries, new_keys, preferred_element_type=jnp.float32)
        * softmax_scale
    )
    new_scores = jnp.where(new_valid, new_scores, NEGATIVE)
    local_max = jnp.maximum(jnp.max(scores, axis=-1), jnp.max(new_scores, axis=-1))
    weights = jnp.where(valid[:, None, None, None, :], jnp.exp(scores - local_max[..., None]), 0.0)
    new_weights = jnp.where(new_valid, jnp.exp(new_scores - local_max[..., None]), 0.0)
    totals = jnp.sum(weights, axis=-1) + jnp.sum(new_weights, axis=-1)
    weighted = jnp.einsum(
        "bskgt,tkd->bskgd",
        weights.astype(jnp.bfloat16),
        values_local,
        preferred_element_type=jnp.float32,
    )
    weighted = weighted + jnp.einsum(
        "bskgt,tbkd->bskgd",
        new_weights.astype(jnp.bfloat16),
        new_values,
        preferred_element_type=jnp.float32,
    )
    global_max = lax.pmax(local_max, "ctx")
    factor = jnp.exp(local_max - global_max)
    totals_all, weighted_all = lax.psum((totals * factor, weighted * factor[..., None]), "ctx")
    attended = (weighted_all / totals_all[..., None]).astype(jnp.bfloat16)
    attended = jnp.transpose(attended, (1, 0, 2, 3, 4)).reshape(
        n_steps * n_reqs, kv_local * group_size * HD
    )
    project_part = jnp.dot(attended, w_out, preferred_element_type=jnp.float32)
    projected = (
        lax.psum(project_part, "head").astype(jnp.bfloat16).reshape(n_steps, n_reqs, width_local)
    )
    complete = lax.all_gather(projected, "ctx", axis=2, tiled=True)
    selector = owned.astype(jnp.bfloat16)
    own_row = jnp.einsum(
        "sbd,b->sd", complete, selector, preferred_element_type=jnp.float32
    ).astype(jnp.bfloat16)
    return own_row[None]


def solution(mesh):
    placed = (
        P(None, None, "ctx"),
        P("ctx"),
        P("ctx", "head"),
        P("ctx", "head"),
        P("head", "ctx"),
        P("ctx", None, "head", None),
        P(),
        P(),
        P(),
    )
    return jax.shard_map(
        body, mesh=mesh, in_specs=placed, out_specs=P("ctx", None, None), check_vma=False
    )
```

profile of v0, /device:TPU:1, one launch (start us, length us, event | category | flops | bytes accessed | tf_op | source)
XLA Modules:
  0.0 702.8 jit_solution(1155721062864921964)
XLA Ops:
  6.5 0.0 copy-start
  6.5 0.0 copy-start.2
  6.5 0.0 all-reduce.3.cloned.1.call-start
  6.5 0.9 fusion.27
  7.5 0.7 convert_element_type.53
  8.2 131.2 %psum.42 = f32[2,4]{1,0:T(2,128)S(1)} all-reduce(f32[2,4]{1,0:T(2,128)S(1)} %fusion.27), channel_id=1, replica_groups=mesh['ctx'=64,'head'=8] {'ctx'}, use_global_device_ids=true, to_apply=%region_3.0 | all-reduce | flops 8 | bytes 64 | tf_op jit(solution)/shard_map/psum | solution.py:39
  139.3 0.8 fusion.26
  140.1 0.0 copy-done
  140.1 0.9 fusion.49
  141.0 0.0 all-reduce.3.cloned.1.call-update
  141.0 0.0 all-reduce.5.cloned.1.call-start
  141.1 0.9 compare_reduce_fusion
  142.0 0.9 fusion.10
  143.0 0.7 broadcast_compare_fusion
  143.6 0.7 add_convert_fusion
  144.3 1.0 fusion.50
  145.4 130.5 %psum.44 = f32[2,4,1,256]{3,0,1,2:T(2,128)S(1)} all-reduce(f32[2,4,1,256]{3,0,1,2:T(2,128)S(1)} %copy.55), channel_id=1, replica_groups=mesh['ctx'=64,'head'=8] {'ctx'}, use_global_device_ids=true, to_apply=%region_6.7 | all-reduce | flops 2048 | bytes 16384 | tf_op jit(solution)/shard_map/psum | solution.py:53
  275.9 0.1 slice_negate_fusion
  275.9 0.1 broadcast_bitcast_fusion.1
  276.0 0.1 broadcast_bitcast_fusion
  276.1 0.1 broadcast_and_fusion
  276.2 0.1 fusion.44
  276.3 0.8 fusion.17
  277.0 0.1 fusion.40
  277.2 41.8 %all-reduce.3.cloned.1.call-done = f32[8,2048]{1,0:T(8,128)} async-done(((f32[8,2048]{1,0:T(8,128)}), f32[8,2048]{1,0:T(8,128)}) %all-reduce.3.cloned.1.call-update) | async-done | bytes 65552 | tf_op jit(solution)/shard_map/psum | solution.py:53
  318.9 0.9 copy.75
  319.8 0.1 fusion.45
  319.9 0.1 maximum_multiply_fusion
  320.0 0.9 fusion.19
  320.9 0.0 copy-done.2
  320.9 0.6 fusion.47
  321.5 0.3 fusion.48
  321.8 0.6 fusion.2
  322.5 124.0 %pmax.7 = f32[4,2,1,16]{3,1,0,2:T(2,128)S(1)} all-reduce(f32[4,2,1,16]{3,1,0,2:T(2,128)S(1)} %bitcast.159), channel_id=1, replica_groups=mesh['ctx'=64,'head'=8] {'ctx'}, use_global_device_ids=true, to_apply=%region_8.9 | all-reduce | flops 128 | bytes 1024 | tf_op jit(solution)/shard_map/pmax | solution.py:107
  446.5 0.1 fusion.43
  446.5 0.0 copy-start.1
  446.6 1.7 convolution_bitcast_fusion.1
  448.3 0.9 fusion.5
  449.2 0.0 all-reduce.5.cloned.1.call-update
  449.3 125.8 %psum.46 = f32[4,2,16]{2,1,0:T(2,128)S(1)} all-reduce(f32[4,2,16]{2,1,0:T(2,128)S(1)} %get-tuple-element.9), channel_id=1, replica_groups=mesh['ctx'=64,'head'=8] {'ctx'}, use_global_device_ids=true, to_apply=%region_12.13 | all-reduce | flops 128 | bytes 1024 | tf_op jit(solution)/shard_map/psum | solution.py:109
  575.1 51.9 %all-reduce.5.cloned.1.call-done = f32[4,2,1,16,128]{4,3,1,0,2:T(8,128)} async-done(((f32[4,2,1,16,128]{4,3,1,0,2:T(8,128)}), f32[4,2,1,16,128]{4,3,1,0,2:T(8,128)}) %all-reduce.5.cloned.1.call-update) | async-done | bytes 65552 | tf_op jit(solution)/shard_map/psum | solution.py:109
  627.0 0.9 fusion.24
  628.0 0.0 copy-done.1
  628.0 0.2 fusion.20
  628.2 13.5 %psum.47 = bf16[8,256]{1,0:T(8,128)(2,1)S(1)} all-reduce(f32[8,256]{1,0:T(8,128)S(1)} %fusion.20), channel_id=1, replica_groups=mesh['ctx'=64,'head'=8] {'head'}, use_global_device_ids=true, to_apply=%region_13.14 | all-reduce | flops 2048 | bytes 12288 | tf_op jit(solution)/shard_map/psum | solution.py:116
  641.7 53.2 %all_gather.3 = bf16[2,4,16384]{2,1,0:T(4,128)(2,1)S(1)} all-gather(bf16[2,4,256]{2,1,0:T(4,128)(2,1)S(1)} %reshape.383), channel_id=1, replica_groups=mesh['ctx'=64,'head'=8] {'ctx'}, dimensions={2}, use_global_device_ids=true | all-gather | bytes 266240 | tf_op jit(solution)/shard_map/all_gather | solution.py:118
  694.9 0.3 fusion.37
  695.2 0.7 copy.118
  (20 shorter events, 0.2 us)
Async XLA Ops:
  6.5 133.6 %copy-start = (bf16[256,2048]{1,0:T(8,128)(2,1)S(1)}, bf16[256,2048]{1,0:T(8,128)(2,1)}, u32[]{:S(2)}) copy-start(bf16[256,2048]{1,0:T(8,128)(2,1)} %param.11) | copy-start | bytes 3145732
  6.5 314.4 %copy-start.2 = (bf16[32,128,1,256]{3,1,2,0:T(8,128)(2,1)S(1)}, bf16[32,128,1,256]{3,1,2,0:T(8,128)(2,1)}, u32[]{:S(2)}) copy-start(bf16[32,128,1,256]{3,1,2,0:T(8,128)(2,1)} %param.14) | copy-start | bytes 6291460
  6.5 312.4 %all-reduce.3.cloned.1.call-start = ((), (), s32[]{:S(2)}) async-start(), calls=%async_computation | async-start | bytes 131072 | tf_op jit(solution)/shard_map/psum | solution.py:53
  141.0 486.0 %all-reduce.5.cloned.1.call-start = ((), (), s32[]{:S(2)}) async-start(), calls=%async_computation.1 | async-start | bytes 131072 | tf_op jit(solution)/shard_map/psum | solution.py:109
  446.5 181.4 %copy-start.1 = (bf16[2048,256]{1,0:T(8,128)(2,1)S(1)}, bf16[2048,256]{1,0:T(8,128)(2,1)}, u32[]{:S(2)}) copy-start(bf16[2048,256]{1,0:T(8,128)(2,1)} %param.13) | copy-start | bytes 3145732
Sparse Core Ops, SparseCore 0:
  141.1 177.7 all-reduce.2
  449.4 177.5 all-reduce.4
where the time goes:
time: 703 us
  blocking collectives  578 us (82%)
  waiting for transfers between devices  93.7 us (13%)
  between operations  13.6 us (2%)
  other arithmetic  9.41 us (1%)
    psum x1, blocking collectives, body(): squares = lax.psum(jnp.sum(hidden_f * hidden_f, axis=-1), 'ctx')  131 us
    psum x1, blocking collectives, body(): query_sum, keyval_sum = lax.psum((query_part, keyval_part), 'ctx')  130 us
    psum x1, blocking collectives, body(): lax.psum((totals * factor, weighted * factor[..., None]), 'ctx')  126 us
    pmax x1, blocking collectives, body(): global_max = lax.pmax(local_max, 'ctx')  124 us
    all_gather x1, blocking collectives, body(): complete = lax.all_gather(projected, 'ctx', axis=2, tiled=True)  53.2 us
    psum x1, waiting for transfers between devices, body(): lax.psum((totals * factor, weighted * factor[..., None]), 'ctx')  51.9 us
    psum x1, waiting for transfers between devices, body(): query_sum, keyval_sum = lax.psum((query_part, keyval_part), 'ctx')  41.8 us
  transfers between devices with their start and end apart: 2, of which 2 were waited for; matrix products, arithmetic and copies ran while one was open for 1% of the time, Pallas kernels for 0%

commit v1 on v0

v1 whole, which is shorter than its diff:
```python
import functools
import math

import jax
import jax.numpy as jnp
from jax import lax
from jax.experimental import pallas as pl
from jax.experimental.pallas import tpu as pltpu
from jax.sharding import PartitionSpec as P

HD = 128
HALF = HD // 2
EPSILON = 1e-05
NEGATIVE = -1e30
FLOOR = -1e29
F32 = jnp.float32
BF16 = jnp.bfloat16


def frequencies(head_size):
    halfway = head_size // 2
    inverse = 500000.0 ** (-(jnp.arange(halfway, dtype=F32) * 2.0 / head_size))
    wavelength = 2.0 * math.pi / inverse
    smooth = (8192.0 / wavelength - 1.0) / 3.0
    blended = (1.0 - smooth) * inverse / 8.0 + smooth * inverse
    return jnp.where(
        wavelength < 2048.0, inverse, jnp.where(wavelength > 8192.0, inverse / 8.0, blended)
    )


def iota(shape, dim):
    return lax.broadcasted_iota(jnp.int32, shape, dim)


def dot(a, b):
    return jnp.dot(a, b, preferred_element_type=F32)


def dot_t(a, b):
    return lax.dot_general(a, b, (((1,), (1,)), ((), ())), preferred_element_type=F32)


def call(kernel, out, scratch=(), n_in=1, smem=()):
    specs = [
        pl.BlockSpec(memory_space=pltpu.SMEM if i in smem else pltpu.VMEM) for i in range(n_in)
    ]
    return pl.pallas_call(
        kernel,
        out_shape=out,
        in_specs=specs,
        out_specs=pl.BlockSpec(memory_space=pltpu.VMEM),
        scratch_shapes=list(scratch),
        compiler_params=pltpu.CompilerParams(vmem_limit_bytes=32 * 1024 * 1024),
    )


def project_kernel(hidden_ref, gain_ref, wq_ref, wkv_ref, out_ref):
    gain = gain_ref[...].astype(F32)
    hid = [hidden_ref[s].astype(F32) for s in range(2)]
    width = hid[0].shape[1]
    row = iota((16, width), 0) % 4
    spread = [
        jnp.concatenate([h[b : b + 1] for b in range(4) for _ in range(4)], axis=0) for h in hid
    ]
    scaled = [x * gain for x in spread]

    def split(x):
        high = x.astype(BF16)
        return high, (x - high.astype(F32)).astype(BF16)

    zero = jnp.zeros_like(scaled[0])
    lhs_q = split(jnp.where(row == 0, scaled[0], jnp.where(row == 1, scaled[1], zero)))
    lhs_q = jnp.concatenate(lhs_q, axis=0)
    lhs_kv = [split(jnp.where(row == 2, x, zero)) for x in scaled]
    lhs_kv = jnp.concatenate([p for pair in lhs_kv for p in pair], axis=0)
    part_kv = dot(lhs_kv, wkv_ref[...])
    part_kv = [part_kv[0:16] + part_kv[16:32], part_kv[32:48] + part_kv[48:64]]
    squares = [jnp.sum(x * x, axis=-1, keepdims=True) for x in spread]
    tile_row = iota((16, HD), 0) % 4
    lane = iota((16, HD), 1)
    square = jnp.where(lane < HALF, squares[0], squares[1])
    square = jnp.where(tile_row == 3, square, 0.0)
    part_q = dot(lhs_q, wq_ref[...])
    part_q = part_q[0:16] + part_q[16:32]
    heads = part_q.shape[1] // HD
    for h in range(heads):
        block = part_q[:, h * HD : (h + 1) * HD] + square
        if h < 4:
            block = block + part_kv[h % 2][:, (h // 2) * HD : (h // 2 + 1) * HD]
        out_ref[h * 16 : (h + 1) * 16, :] = block


def finish_kernel(inverse_width, parts_ref, cos_ref, sin_ref, first_ref, out_ref):
    n = parts_ref.shape[0]
    total = parts_ref[0:8, :]
    for k in range(1, n // 8):
        total = total + parts_ref[k * 8 : (k + 1) * 8, :]
    total = total + pltpu.roll(total, 4, 0)
    root = lax.rsqrt(total * inverse_width + EPSILON)
    root0 = root[3:4, 0:1]
    root1 = root[3:4, HALF : HALF + 1]
    scaled = total * jnp.where(first_ref[...] > 0.5, root0, root1)
    turned = scaled * cos_ref[...] + pltpu.roll(scaled, HALF, 1) * sin_ref[...]
    twice = jnp.concatenate([turned, turned], axis=0).astype(BF16)
    for k in range(n // 16):
        out_ref[k * 16 : (k + 1) * 16, :] = twice


def attend_kernel(scale, rows_ref, limit_ref, cache_ref, out_ref, flat_ref, score_ref):
    flat_ref[...] = rows_ref[...].astype(F32)
    peers = flat_ref.shape[0] // 4
    rows = 2 * peers
    query = jnp.concatenate(
        [flat_ref[pl.ds(i, peers, stride=4), :] for i in range(2)], axis=0
    ).astype(BF16)
    new = flat_ref[pl.ds(2, 16, stride=4), :]
    new_keys = new.astype(BF16)
    new_values = pltpu.roll(new, 8, 0).astype(BF16)
    tokens = cache_ref.shape[0]
    page = HD
    lane8 = iota((8, page), 1)
    chunk = 4 * page

    row = iota((rows, 16), 0)
    col = iota((rows, 16), 1)
    new_ok = (
        (col < 8) & (col % 4 == row % 4) & (col // 4 <= row // peers)
    ) & (limit_ref[0:1, page - 1 : page] > 0)
    new_scores = jnp.where(new_ok, dot_t(query, new_keys) * scale, NEGATIVE)

    best = None
    for start in range(0, tokens, chunk):
        part = dot_t(query, cache_ref[start : start + chunk, 0:HD]) * scale
        for k in range(chunk // page):
            p = start // page + k
            ok = lane8 < limit_ref[:, p : p + 1]
            piece = part[:, k * page : (k + 1) * page].reshape(rows // 8, 8, page)
            piece = jnp.where(ok[None], piece, NEGATIVE).reshape(rows, page)
            score_ref[:, start + k * page : start + (k + 1) * page] = piece
            best = piece if best is None else jnp.maximum(best, piece)
    top = jnp.maximum(
        jnp.max(best, axis=-1, keepdims=True), jnp.max(new_scores, axis=-1, keepdims=True)
    )
    top = jnp.maximum(top, FLOOR)
    new_weights = jnp.exp(new_scores - top)
    total = jnp.sum(new_weights, axis=-1, keepdims=True)
    mixed = dot(new_weights.astype(BF16), new_values)
    sums = jnp.zeros((rows, page), F32)
    for start in range(0, tokens, chunk):
        weights = jnp.exp(score_ref[:, start : start + chunk] - top)
        for k in range(chunk // page):
            sums = sums + weights[:, k * page : (k + 1) * page]
        mixed = mixed + dot(weights.astype(BF16), cache_ref[start : start + chunk, HD : 2 * HD])
    total = total + jnp.sum(sums, axis=-1, keepdims=True)
    stats = jnp.where(iota((rows, HD), 1) < HALF, top, total)
    for i in range(2):
        out_ref[pl.ds(i, peers, stride=4), :] = mixed[i * peers : (i + 1) * peers]
        out_ref[pl.ds(2 + i, peers, stride=4), :] = stats[i * peers : (i + 1) * peers]


def merge_kernel(parts_ref, out_ref):
    peers = parts_ref.shape[0] // 4
    results = []
    for i in range(2):
        mixed = parts_ref[pl.ds(i, peers, stride=4), :]
        stats = parts_ref[pl.ds(2 + i, peers, stride=4), :]
        top = stats[:, 0:1]
        factor = jnp.exp(top - jnp.max(top, axis=0, keepdims=True))
        total = jnp.sum(factor * stats[:, HALF : HALF + 1], axis=0, keepdims=True)
        results.append(jnp.sum(factor * mixed, axis=0, keepdims=True) / total)
    tile = jnp.where(iota((16, HD), 0) % 2 == 0, results[0], results[1]).astype(BF16)
    for k in range(out_ref.shape[0] // 16):
        out_ref[k * 16 : (k + 1) * 16, :] = tile


def output_kernel(rows_ref, w_ref, out_ref):
    rows = rows_ref[...].astype(F32)
    heads = rows.shape[0] // 8
    lhs = jnp.concatenate([rows[h * 8 : (h + 1) * 8] for h in range(heads)], axis=1)
    part = dot(lhs.astype(BF16), w_ref[...])
    for k in range(out_ref.shape[0] // 8):
        out_ref[k * 8 : (k + 1) * 8, :] = part


def deliver_kernel(owners_ref, parts_ref, out_ref):
    total = parts_ref[0:8, :]
    for k in range(1, parts_ref.shape[0] // 8):
        total = total + parts_ref[k * 8 : (k + 1) * 8, :]
    n = out_ref.shape[0]
    row = iota((n, HD), 0)
    slot = row // 4
    result = jnp.zeros((n, HD), F32)
    small = iota((8, HD), 0)
    for b in range(4):
        tile = jnp.zeros((8, HD), F32)
        for ct in range(2):
            for s in range(2):
                piece = total[2 * b + s : 2 * b + s + 1, ct * HD : (ct + 1) * HD]
                tile = jnp.where(small % 4 == 2 * ct + s, piece, tile)
        spread = jnp.concatenate([tile] * (n // 8), axis=0)
        result = jnp.where(slot == owners_ref[b], spread, result)
    out_ref[...] = result.astype(BF16)


def body(hidden, norm_gain, w_query, w_keyval, w_out, cache, page_table, lengths, owners):
    n_steps, n_reqs, width_local = hidden.shape
    peers = lax.axis_size("ctx")
    groups = lax.axis_size("head")
    device_now = lax.axis_index("ctx")
    width_total = width_local * peers
    pages, page_len = cache.shape[0], cache.shape[1]

    def exchange(x, axis):
        return lax.all_to_all(x, axis, 0, 0, tiled=True)

    request = device_now % n_reqs
    head = device_now // n_reqs
    kv_step = head % 2
    steps = jnp.stack([jnp.int32(0), jnp.int32(1), kv_step, jnp.int32(0)])
    steps = jnp.concatenate([steps, steps])
    position = (lengths[request] + steps).astype(F32)
    angles = position[:, None] * frequencies(HD)
    turns = jnp.concatenate([steps[:2] * 0 + 1, jnp.stack([(head < 2).astype(jnp.int32), 0])])
    turns = jnp.concatenate([turns, turns])[:, None] > 0
    cosine = jnp.where(turns, jnp.cos(angles), 1.0)
    sine = jnp.where(turns, jnp.sin(angles), 0.0)
    cosine = jnp.concatenate([cosine, cosine], axis=-1)
    sine = jnp.concatenate([-sine, sine], axis=-1)
    first = jnp.broadcast_to((steps == 0).astype(F32)[:, None], (8, HD))

    global_ids = device_now * pages + jnp.arange(pages, dtype=jnp.int32)
    logical = jnp.arange(page_table.shape[1], dtype=jnp.int32)
    in_page = jnp.clip(lengths[:, None] - logical[None, :] * page_len, 0, page_len)
    limit = jnp.sum(
        jnp.where(page_table[:, :, None] == global_ids[None, None, :], in_page[:, :, None], 0),
        axis=1,
    )
    limit = jnp.pad(
        limit, ((0, 0), (0, HD - 1 - pages))
    )
    flag = jnp.broadcast_to((device_now == 0).astype(jnp.int32), (n_reqs, 1))
    limit = jnp.concatenate([limit, flag], axis=1)
    limit = jnp.concatenate([limit, limit], axis=0)

    with jax.named_scope("project"):
        parts = call(
            project_kernel, jax.ShapeDtypeStruct((4 * peers, HD), F32), n_in=4
        )(hidden, norm_gain.reshape(1, width_local), w_query, w_keyval)
    parts = exchange(parts.reshape(peers, 4, HD), "ctx").reshape(4 * peers, HD)
    with jax.named_scope("finish"):
        rows = call(
            functools.partial(finish_kernel, 1.0 / width_total),
            jax.ShapeDtypeStruct((4 * peers, HD), BF16),
            n_in=4,
        )(parts, cosine, sine, first)
    rows = exchange(rows.reshape(peers, 4, HD), "ctx").reshape(4 * peers, HD)
    tokens = cache.reshape(pages * page_len, 2 * HD)
    with jax.named_scope("attend"):
        parts = call(
            functools.partial(attend_kernel, HD ** (-0.5)),
            jax.ShapeDtypeStruct((4 * peers, HD), F32),
            scratch=[
                pltpu.VMEM((4 * peers, HD), F32),
                pltpu.VMEM((2 * peers, pages * page_len), F32),
            ],
            n_in=3,
        )(rows, limit, tokens)
    parts = exchange(parts.reshape(peers, 4, HD), "ctx").reshape(4 * peers, HD)
    with jax.named_scope("merge"):
        rows = call(merge_kernel, jax.ShapeDtypeStruct((2 * peers, HD), BF16), n_in=1)(parts)
    rows = exchange(rows.reshape(peers, 2, HD), "ctx").reshape(2 * peers, HD)
    with jax.named_scope("output"):
        parts = call(
            output_kernel, jax.ShapeDtypeStruct((8 * groups, width_local), F32), n_in=2
        )(rows, w_out)
    parts = exchange(parts.reshape(groups, 8, width_local), "head")
    with jax.named_scope("deliver"):
        sent = call(
            deliver_kernel, jax.ShapeDtypeStruct((4 * peers, HD), BF16), n_in=2, smem=(0,)
        )(owners, parts.reshape(8 * groups, width_local))
    got = exchange(sent.reshape(peers, 4, HD), "ctx")
    got = got.reshape(peers, width_local // HD, n_steps, HD)
    return jnp.transpose(got, (2, 0, 1, 3)).reshape(1, n_steps, width_total)


def solution(mesh):
    placed = (
        P(None, None, "ctx"),
        P("ctx"),
        P("ctx", "head"),
        P("ctx", "head"),
        P("head", "ctx"),
        P("ctx", None, "head", None),
        P(),
        P(),
        P(),
    )
    return jax.shard_map(
        body, mesh=mesh, in_specs=placed, out_specs=P("ctx", None, None), check_vma=False
    )
```

time: 703 us -> 107 us (0.15)
  blocking collectives: 578 us -> 57.4 us
  waiting for transfers between devices: 93.7 us -> 17.3 us
  starting transfers between devices: 0.04 us -> 19.5 us
  between operations: 13.6 us -> 0.14 us
    psum x4 -> x0, blocking collectives: 401 us -> none  [the longest x1 131 us: body(): squares = lax.psum(jnp.sum(hidden_f * hidden_f, axis=-1), 'ctx')]
    pmax x1 -> x0, blocking collectives: 124 us -> none  [body(): global_max = lax.pmax(local_max, 'ctx')]
    psum x2 -> x0, waiting for transfers between devices: 93.7 us -> none  [the longest x1 51.9 us: body(): lax.psum((totals * factor, weighted * factor[..., None]), 'ctx')]
    all_to_all x0 -> x4, blocking collectives: none -> 57.4 us  [exchange(): return lax.all_to_all(x, axis, 0, 0, tiled=True)]
    all_gather x1 -> x0, blocking collectives: 53.2 us -> none  [body(): complete = lax.all_gather(projected, 'ctx', axis=2, tiled=True)]
    all_to_all x0 -> x2, starting transfers between devices: none -> 19.5 us  [exchange(): return lax.all_to_all(x, axis, 0, 0, tiled=True)]
    all_to_all x0 -> x2, waiting for transfers between devices: none -> 17.3 us  [exchange(): return lax.all_to_all(x, axis, 0, 0, tiled=True)]
  transfers between devices with their start and end apart: 2 -> 2, of which waited for: 2 -> 2; matrix products, arithmetic and copies ran while one was open for 1% -> 4% of each run, Pallas kernels for 0% -> 0%
where the time goes in v1:
time: 107 us
  blocking collectives  57.4 us (54%)
  starting transfers between devices  19.5 us (18%)
  waiting for transfers between devices  17.3 us (16%)
  local copies, waits for them, and re-layouts  5.77 us (5%)
  Pallas kernels  4.11 us (4%)
  other arithmetic  2.42 us (2%)
    all_to_all x4, blocking collectives, exchange(): return lax.all_to_all(x, axis, 0, 0, tiled=True)  57.4 us
    all_to_all x2, starting transfers between devices, exchange(): return lax.all_to_all(x, axis, 0, 0, tiled=True)  19.5 us
    all_to_all x2, waiting for transfers between devices, exchange(): return lax.all_to_all(x, axis, 0, 0, tiled=True)  17.3 us
    unnamed x12, local copies, waits for them, and re-layouts  2.83 us
  transfers between devices with their start and end apart: 2, of which 2 were waited for; matrix products, arithmetic and copies ran while one was open for 4% of the time, Pallas kernels for 0%

profile of v1, /device:TPU:1, one launch (start us, length us, event | category | flops | bytes accessed | tf_op | source)
XLA Modules:
  0.0 106.7 jit_solution(2100916915062277199)
XLA Ops:
  0.0 0.0 copy-start
  0.0 0.8 reshape.252.gain_ref
  0.8 0.0 copy-start.1
  0.8 1.2 %copy-done.1 = bf16[256,2048]{1,0:T(8,128)(2,1)S(1)} copy-done((bf16[256,2048]{1,0:T(8,128)(2,1)S(1)}, bf16[256,2048]{1,0:T(8,128)(2,1)}, u32[]{:S(2)}) %copy-start.1) | copy-done | bytes 1048600
  2.0 0.0 copy-start.3
  2.0 0.9 copy-done.3
  2.9 0.0 copy-start.4
  2.9 0.7 copy-done.4
  3.6 1.0 project.1
  4.6 0.0 copy-start.2
  4.6 15.0 %all-to-all-start = ((f32[64,4,128]{2,1,0:T(4,128)}), f32[64,4,128]{2,1,0:T(4,128)S(1)}, u32[]{:S(2)}, u32[]{:S(2)}) async-start(f32[64,4,128]{2,1,0:T(4,128)} %bitcast), calls=%async_computation | async-start | bytes 262144 | tf_op jit(solution)/shard_map/all_to_all | solution.py:214
  19.7 0.1 concatenate.44
  19.7 1.2 %dynamic_slice.3 = s32[1]{0:T(128)} dynamic-slice(s32[4]{0:T(128)} %param.16, s32[]{:T(128)S(6)} %select_n.46), dynamic_slice_sizes={1} | dynamic-slice | bytes 12 | tf_op jit(solution)/shard_map/dynamic_slice | solution.py:221
  21.0 0.7 subtract_clamp_fusion
  21.7 0.1 concatenate.46
  21.8 0.6 add_convert_fusion
  22.3 0.1 fusion.2
  22.4 0.9 select_reduce_fusion
  23.4 0.1 pad_maximum_fusion
  23.4 7.2 %all-to-all-done = f32[64,4,128]{2,1,0:T(4,128)S(1)} async-done(((f32[64,4,128]{2,1,0:T(4,128)}), f32[64,4,128]{2,1,0:T(4,128)S(1)}, u32[]{:S(2)}, u32[]{:S(2)}) %all-to-all-start) | async-done | bytes 131104 | tf_op jit(solution)/shard_map/all_to_all | solution.py:214
  30.7 0.1 broadcast_in_dim.48.first_ref
  30.8 0.9 finish.1
  31.6 0.0 copy-start.5
  31.6 4.6 %all-to-all-start.1 = ((bf16[64,4,128]{2,1,0:T(4,128)(2,1)}), bf16[64,4,128]{2,1,0:T(4,128)(2,1)S(1)}, u32[]{:S(2)}, u32[]{:S(2)}) async-start(bf16[64,4,128]{2,1,0:T(4,128)(2,1)} %bitcast.5), calls=%async_computation.1 | async-start | bytes 131072 | tf_op jit(solution)/shard_map/all_to_all | solution.py:214
  36.2 10.1 %all-to-all-done.1 = bf16[64,4,128]{2,1,0:T(4,128)(2,1)S(1)} async-done(((bf16[64,4,128]{2,1,0:T(4,128)(2,1)}), bf16[64,4,128]{2,1,0:T(4,128)(2,1)S(1)}, u32[]{:S(2)}, u32[]{:S(2)}) %all-to-all-start.1) | async-done | bytes 65568 | tf_op jit(solution)/shard_map/all_to_all | solution.py:214
  46.3 0.0 copy-done
  46.3 1.3 %attend.1 = f32[256,128]{1,0:T(8,128)S(1)} custom-call(bf16[256,128]{1,0:T(8,128)(2,1)S(1)} %bitcast.23, s32[8,128]{1,0:T(8,128)S(1)} %pad_add_fusion.limit_ref, bf16[4096,256]{1,0:T(8,128)(2,1)S(1)} %bitcast.19), custom_call_target="tpu_custom_call" | custom-call | tf_op jit(solution)/shard_map/attend/pallas_call | solution.py:259
  47.6 15.0 %all_to_all.30 = f32[64,4,128]{2,1,0:T(4,128)S(1)} all-to-all(f32[64,4,128]{2,1,0:T(4,128)S(1)} %bitcast.20), channel_id=1, replica_groups=mesh['ctx'=64,'head'=8] {'ctx'}, dimensions={0} | all-to-all | bytes 262144 | tf_op jit(solution)/shard_map/all_to_all | solution.py:214
  62.6 0.2 merge.1
  62.8 13.1 %all_to_all.31 = bf16[64,2,128]{2,1,0:T(2,128)(2,1)S(1)} all-to-all(bf16[64,2,128]{2,1,0:T(2,128)(2,1)S(1)} %bitcast.27), channel_id=1, replica_groups=mesh['ctx'=64,'head'=8] {'ctx'}, dimensions={0} | all-to-all | bytes 65536 | tf_op jit(solution)/shard_map/all_to_all | solution.py:214
  75.9 0.0 copy-done.2
  75.9 0.2 output.1
  76.1 13.9 %all_to_all.32 = f32[8,8,256]{2,1,0:T(8,128)S(1)} all-to-all(f32[8,8,256]{2,1,0:T(8,128)S(1)} %bitcast.24), channel_id=1, replica_groups=mesh['ctx'=64,'head'=8] {'head'}, dimensions={0} | all-to-all | bytes 131072 | tf_op jit(solution)/shard_map/all_to_all | solution.py:214
  90.0 0.0 copy-done.5
  90.0 0.6 deliver.1
  90.6 15.5 %all_to_all.33 = bf16[64,4,128]{2,1,0:T(4,128)(2,1)S(1)} all-to-all(bf16[64,4,128]{2,1,0:T(4,128)(2,1)S(1)} %bitcast.26), channel_id=1, replica_groups=mesh['ctx'=64,'head'=8] {'ctx'}, dimensions={0} | all-to-all | bytes 131072 | tf_op jit(solution)/shard_map/all_to_all | solution.py:214
  106.1 0.7 reshape.266
  (9 shorter events, 0.1 us)
Async XLA Ops:
  0.0 46.3 %copy-start = (bf16[32,128,1,256]{3,1,2,0:T(8,128)(2,1)S(1)}, bf16[32,128,1,256]{3,1,2,0:T(8,128)(2,1)}, u32[]{:S(2)}) copy-start(bf16[32,128,1,256]{3,1,2,0:T(8,128)(2,1)} %param.14) | copy-start | bytes 6291460
  0.8 1.2 %copy-start.1 = (bf16[256,2048]{1,0:T(8,128)(2,1)S(1)}, bf16[256,2048]{1,0:T(8,128)(2,1)}, u32[]{:S(2)}) copy-start(bf16[256,2048]{1,0:T(8,128)(2,1)} %wq_ref.1) | copy-start | bytes 3145732
  2.0 0.9 copy-start.3
  2.9 0.7 copy-start.4
  4.6 71.3 %copy-start.2 = (bf16[2048,256]{1,0:T(8,128)(2,1)S(1)}, bf16[2048,256]{1,0:T(8,128)(2,1)}, u32[]{:S(2)}) copy-start(bf16[2048,256]{1,0:T(8,128)(2,1)} %w_ref.1) | copy-start | bytes 3145732
  4.6 26.1 %all-to-all-start = ((f32[64,4,128]{2,1,0:T(4,128)}), f32[64,4,128]{2,1,0:T(4,128)S(1)}, u32[]{:S(2)}, u32[]{:S(2)}) async-start(f32[64,4,128]{2,1,0:T(4,128)} %bitcast), calls=%async_computation | async-start | bytes 262144 | tf_op jit(solution)/shard_map/all_to_all | solution.py:214
  31.6 58.4 %copy-start.5 = (s32[4]{0:T(128)S(1)}, s32[4]{0:T(128)}, u32[]{:S(2)}) copy-start(s32[4]{0:T(128)} %owners_ref.1) | copy-start | bytes 52
  31.6 14.7 %all-to-all-start.1 = ((bf16[64,4,128]{2,1,0:T(4,128)(2,1)}), bf16[64,4,128]{2,1,0:T(4,128)(2,1)S(1)}, u32[]{:S(2)}, u32[]{:S(2)}) async-start(bf16[64,4,128]{2,1,0:T(4,128)(2,1)} %bitcast.5), calls=%async_computation.1 | async-start | bytes 131072 | tf_op jit(solution)/shard_map/all_to_all | solution.py:214

commit v2 on v1

v2 whole, which is shorter than its diff:
```python
import functools
import math

import jax
import jax.numpy as jnp
import numpy as np
from jax import lax
from jax.experimental import pallas as pl
from jax.experimental.pallas import tpu as pltpu
from jax.sharding import Mesh, PartitionSpec as P

HD = 128
HALF = HD // 2
EPSILON = 1e-05
NEGATIVE = -1e30
FLOOR = -1e29
F32 = jnp.float32
BF16 = jnp.bfloat16


def frequencies(head_size):
    index = np.arange(head_size // 2)
    inverse = 500000.0 ** (-2.0 * index / head_size)
    wavelength = 2.0 * math.pi / inverse
    smooth = (8192.0 / wavelength - 1.0) / 3.0
    blended = (1.0 - smooth) * inverse / 8.0 + smooth * inverse
    chosen = np.where(
        wavelength < 2048.0, inverse, np.where(wavelength > 8192.0, inverse / 8.0, blended)
    )
    return chosen.astype(np.float32)


def iota(shape, dim):
    return lax.broadcasted_iota(jnp.int32, shape, dim)


def dot(a, b):
    return jnp.dot(a, b, preferred_element_type=F32)


def dot_t(a, b):
    return lax.dot_general(a, b, (((1,), (1,)), ((), ())), preferred_element_type=F32)


def call(kernel, out, spaces, scratch=(), limit=24):
    return pl.pallas_call(
        kernel,
        out_shape=out,
        in_specs=[pl.BlockSpec(memory_space=space) for space in spaces],
        out_specs=pl.BlockSpec(memory_space=pltpu.VMEM),
        scratch_shapes=list(scratch),
        compiler_params=pltpu.CompilerParams(vmem_limit_bytes=limit * 1024 * 1024),
    )


def split2(x):
    high = x.astype(BF16)
    return high, (x - high.astype(F32)).astype(BF16)


def split3(x):
    first = x.astype(BF16).astype(F32)
    rest = x - first
    second = rest.astype(BF16).astype(F32)
    return first, second, rest - second


def project_kernel(
    hidden_hbm, gain_hbm, wq_hbm, wkv_hbm, out_ref, hidden_ref, gain_ref, wq_ref, wkv_ref, sems
):
    chunks = sems.shape[0] - 3
    chunk = wq_ref.shape[1] // chunks
    copies = [
        pltpu.make_async_copy(hidden_hbm, hidden_ref, sems.at[0]),
        pltpu.make_async_copy(gain_hbm, gain_ref, sems.at[1]),
        pltpu.make_async_copy(wkv_hbm, wkv_ref, sems.at[2]),
    ]
    for k in range(chunks):
        cols = pl.ds(k * chunk, chunk)
        copies.append(
            pltpu.make_async_copy(wq_hbm.at[:, cols], wq_ref.at[:, cols], sems.at[3 + k])
        )
    for copy in copies:
        copy.start()
    copies[0].wait()
    copies[1].wait()
    gain = gain_ref[...].astype(F32).reshape(1, gain_ref.shape[0])
    hid = [hidden_ref[s].astype(F32) for s in range(2)]
    width = hid[0].shape[1]
    row = iota((16, width), 0) % 4
    spread = [
        jnp.concatenate([h[b : b + 1] for b in range(4) for _ in range(4)], axis=0) for h in hid
    ]
    scaled = [x * gain for x in spread]
    zero = jnp.zeros_like(scaled[0])
    lhs_q = split2(jnp.where(row == 0, scaled[0], jnp.where(row == 1, scaled[1], zero)))
    lhs_q = jnp.concatenate(lhs_q, axis=0)
    lhs_kv = [split2(jnp.where(row == 2, x, zero)) for x in scaled]
    lhs_kv = jnp.concatenate([p for pair in lhs_kv for p in pair], axis=0)
    squares = [jnp.sum(x * x, axis=-1, keepdims=True) for x in spread]
    square = jnp.where(iota((16, HD), 1) < HALF, squares[0], squares[1])
    square = jnp.where(iota((16, HD), 0) % 4 == 3, square, 0.0)
    copies[2].wait()
    part_kv = dot(lhs_kv, wkv_ref[...])
    part_kv = [part_kv[0:16] + part_kv[16:32], part_kv[32:48] + part_kv[48:64]]
    for k in range(chunks):
        copies[3 + k].wait()
        part_q = dot(lhs_q, wq_ref[:, k * chunk : (k + 1) * chunk])
        part_q = part_q[0:16] + part_q[16:32]
        for g in range(chunk // HD):
            h = k * (chunk // HD) + g
            block = part_q[:, g * HD : (g + 1) * HD] + square
            if h < 4:
                block = block + part_kv[h % 2][:, (h // 2) * HD : (h // 2 + 1) * HD]
            out_ref[h * 16 : (h + 1) * 16, :] = block


def finish_kernel(inverse_width, parts_ref, cos_ref, sin_ref, first_ref, out_ref):
    n = parts_ref.shape[0]
    total = parts_ref[0:8, :]
    for k in range(1, n // 8):
        total = total + parts_ref[k * 8 : (k + 1) * 8, :]
    total = total + pltpu.roll(total, 4, 0)
    root = lax.rsqrt(total * inverse_width + EPSILON)
    root0 = root[3:4, 0:1]
    root1 = root[3:4, HALF : HALF + 1]
    scaled = total * jnp.where(first_ref[...] > 0.5, root0, root1)
    turned = scaled * cos_ref[...] + pltpu.roll(scaled, HALF, 1) * sin_ref[...]
    twice = jnp.concatenate([turned, turned], axis=0).astype(BF16)
    for k in range(n // 16):
        out_ref[k * 16 : (k + 1) * 16, :] = twice


def attend_kernel(scale, rows_ref, limit_ref, keys_ref, values_ref, out_ref, flat_ref, score_ref):
    flat_ref[...] = rows_ref[...].astype(F32)
    peers = flat_ref.shape[0] // 4
    rows = 2 * peers
    query = jnp.concatenate(
        [flat_ref[pl.ds(i, peers, stride=4), :] for i in range(2)], axis=0
    ).astype(BF16)
    new = flat_ref[pl.ds(2, 16, stride=4), :]
    new_keys = new.astype(BF16)
    new_values = pltpu.roll(new, 8, 0).astype(BF16)
    tokens = keys_ref.shape[0]
    page = HD
    lane8 = iota((8, page), 1)
    chunk = 4 * page

    row = iota((rows, 16), 0)
    col = iota((rows, 16), 1)
    new_ok = (
        (col < 8) & (col % 4 == row % 4) & (col // 4 <= row // peers)
    ) & (limit_ref[0:1, page - 1 : page] > 0)
    new_scores = jnp.where(new_ok, dot_t(query, new_keys) * scale, NEGATIVE)

    best = None
    for start in range(0, tokens, chunk):
        part = dot_t(query, keys_ref[start : start + chunk, :]) * scale
        for k in range(chunk // page):
            p = start // page + k
            ok = lane8 < limit_ref[:, p : p + 1]
            piece = part[:, k * page : (k + 1) * page].reshape(rows // 8, 8, page)
            piece = jnp.where(ok[None], piece, NEGATIVE).reshape(rows, page)
            score_ref[:, start + k * page : start + (k + 1) * page] = piece
            best = piece if best is None else jnp.maximum(best, piece)
    top = jnp.maximum(
        jnp.max(best, axis=-1, keepdims=True), jnp.max(new_scores, axis=-1, keepdims=True)
    )
    top = jnp.maximum(top, FLOOR)
    new_weights = jnp.exp(new_scores - top)
    total = jnp.sum(new_weights, axis=-1, keepdims=True)
    mixed = dot(new_weights.astype(BF16), new_values)
    sums = jnp.zeros((rows, page), F32)
    for start in range(0, tokens, chunk):
        weights = jnp.exp(score_ref[:, start : start + chunk] - top)
        for k in range(chunk // page):
            sums = sums + weights[:, k * page : (k + 1) * page]
        pair = jnp.concatenate(split2(weights), axis=0)
        pair = dot(pair, values_ref[start : start + chunk, :])
        mixed = mixed + pair[:rows] + pair[rows:]
    total = total + jnp.sum(sums, axis=-1, keepdims=True)
    post(mixed, top, total, out_ref)


STATS = 16


def post(mixed, top, total, out_ref):
    rows = mixed.shape[0]
    lane = iota((rows, HD), 1)
    stats = jnp.zeros((rows, HD), F32)
    for k, piece in enumerate(split3(top) + split3(total)):
        stats = jnp.where(lane == k, piece, stats)
    stats = jnp.transpose(stats)[0:STATS].astype(BF16)
    mixed = mixed.astype(BF16)
    block = rows + STATS
    for k in range(out_ref.shape[0] // block):
        out_ref[k * block : k * block + rows, :] = mixed
        out_ref[k * block + rows : (k + 1) * block, :] = stats


def merge(parts_ref):
    rows = HD
    block = rows + STATS
    peers = parts_ref.shape[0] // block
    stats = jnp.concatenate(
        [parts_ref[k * block + rows : (k + 1) * block, :].astype(F32) for k in range(peers)],
        axis=0,
    )
    stats = jnp.transpose(stats)
    stats = stats + pltpu.roll(stats, HD - 1, 1) + pltpu.roll(stats, HD - 2, 1)
    leading = iota((rows, HD), 1) % STATS == 0
    top = jnp.max(jnp.where(leading, stats, NEGATIVE), axis=-1, keepdims=True)
    factor = jnp.where(leading, jnp.exp(jnp.where(leading, stats, top) - top), 0.0)
    total = jnp.sum(factor * pltpu.roll(stats, HD - 3, 1), axis=-1, keepdims=True)
    mixed = jnp.zeros((rows, HD), F32)
    for k in range(peers):
        part = parts_ref[k * block : k * block + rows, :].astype(F32)
        mixed = mixed + factor[:, k * STATS : k * STATS + 1] * part
    return mixed, top, total


def merge_kernel(parts_ref, out_ref):
    mixed, top, total = merge(parts_ref)
    post(mixed, top, total, out_ref)


def output_kernel(parts_ref, w_ref, out_ref):
    mixed, _, total = merge(parts_ref)
    rows = mixed / total
    half = rows.shape[0] // 2
    lhs = jnp.concatenate(
        [
            jnp.concatenate([rows[i * half + h * 4 : i * half + h * 4 + 4] for i in range(2)], axis=0)
            for h in range(half // 4)
        ],
        axis=1,
    )
    part = dot(lhs.astype(BF16), w_ref[...])
    for k in range(out_ref.shape[0] // 8):
        out_ref[k * 8 : (k + 1) * 8, :] = part


def deliver_kernel(owners_ref, parts_ref, out_ref):
    total = parts_ref[0:8, :]
    for k in range(1, parts_ref.shape[0] // 8):
        total = total + parts_ref[k * 8 : (k + 1) * 8, :]
    width = total.shape[1]
    out_ref[...] = jnp.zeros_like(out_ref)
    for b in range(4):
        pair = jnp.concatenate([total[b : b + 1], total[4 + b : 5 + b]], axis=0).astype(BF16)
        place = pl.multiple_of(owners_ref[b] * width, width)
        out_ref[:, pl.ds(place, width)] = pair


def body(hidden, norm_gain, w_query, w_keyval, w_out, cache, page_table, lengths, owners):
    n_steps, n_reqs, width_local = hidden.shape
    ctx = ("z", "xc")
    far, near = lax.axis_size("z"), lax.axis_size("xc")
    peers = far * near
    groups = lax.axis_size("head")
    device_now = lax.axis_index(ctx)
    width_total = width_local * peers
    pages, page_len = cache.shape[0], cache.shape[1]
    vmem, hbm, smem = pltpu.VMEM, pl.ANY, pltpu.SMEM

    def exchange(x, axis, dim=0):
        return lax.all_to_all(x, axis, dim, dim, tiled=True)

    with jax.named_scope("project"):
        chunks = 4
        parts = call(
            project_kernel,
            jax.ShapeDtypeStruct((4 * peers, HD), F32),
            [hbm] * 4,
            scratch=[
                pltpu.VMEM(hidden.shape, BF16),
                pltpu.VMEM(norm_gain.shape, BF16),
                pltpu.VMEM(w_query.shape, BF16),
                pltpu.VMEM(w_keyval.shape, BF16),
                pltpu.SemaphoreType.DMA((chunks + 3,)),
            ],
            limit=60,
        )(hidden, norm_gain, w_query, w_keyval)
    parts, lengths, page_table, cache = lax.optimization_barrier(
        (parts, lengths, page_table, cache)
    )
    parts = exchange(parts.reshape(peers, 4, HD), ctx).reshape(4 * peers, HD)

    request = lax.rem(device_now, n_reqs)
    head = lax.div(device_now, n_reqs)
    kv_step = lax.rem(head, 2)
    row = lax.broadcasted_iota(jnp.int32, (8, HD), 0) % 4
    steps = jnp.where(row == 1, 1, jnp.where(row == 2, kv_step, 0))
    turns = (row < 2) | ((row == 2) & (head < 2))
    near_length = lax.dynamic_slice(lengths, (request,), (1,))[0]
    position = (near_length + steps).astype(F32)
    freq = np.concatenate([frequencies(HD)] * 2)
    sign = np.concatenate([-np.ones(HALF, np.float32), np.ones(HALF, np.float32)])
    angles = position * freq[None, :]
    cosine = jnp.where(turns, jnp.cos(angles), 1.0)
    sine = jnp.where(turns, jnp.sin(angles) * sign[None, :], 0.0)
    first = (steps == 0).astype(F32)

    lane = np.arange(HD, dtype=np.int32)
    global_ids = jnp.where(lane < pages, device_now * pages + lane, -2)
    logical = np.arange(page_table.shape[1], dtype=np.int32)
    in_page = jnp.clip(lengths[:, None] - logical[None, :] * page_len, 0, page_len)
    limit = jnp.sum(
        jnp.where(page_table[:, :, None] == global_ids[None, None, :], in_page[:, :, None], 0),
        axis=1,
    )
    limit = limit + jnp.where(lane == HD - 1, (device_now == 0).astype(jnp.int32), 0)[None]
    limit = jnp.concatenate([limit, limit], axis=0)
    tokens = cache.reshape(pages * page_len, 2 * HD)
    keys, values = tokens[:, :HD], tokens[:, HD:]
    parts, cosine, sine, first, limit, keys, values = lax.optimization_barrier(
        (parts, cosine, sine, first, limit, keys, values)
    )

    with jax.named_scope("finish"):
        rows = call(
            functools.partial(finish_kernel, 1.0 / width_total),
            jax.ShapeDtypeStruct((4 * peers, HD), BF16),
            [vmem] * 4,
        )(parts, cosine, sine, first)
    rows = exchange(rows.reshape(peers, 4, HD), ctx).reshape(4 * peers, HD)
    block = 2 * peers + STATS
    with jax.named_scope("attend"):
        parts = call(
            functools.partial(attend_kernel, HD ** (-0.5)),
            jax.ShapeDtypeStruct((near * block, HD), BF16),
            [vmem] * 4,
            scratch=[
                pltpu.VMEM((4 * peers, HD), F32),
                pltpu.VMEM((2 * peers, pages * page_len), F32),
            ],
        )(rows, limit, keys, values)
    parts = exchange(parts.reshape(near, block, HD), "xc").reshape(near * block, HD)
    with jax.named_scope("merge"):
        parts = call(
            merge_kernel, jax.ShapeDtypeStruct((far * block, HD), BF16), [vmem]
        )(parts)
    parts = exchange(parts.reshape(far, block, HD), "z").reshape(far * block, HD)
    with jax.named_scope("output"):
        parts = call(
            output_kernel,
            jax.ShapeDtypeStruct((8 * groups, width_local), F32),
            [vmem] * 2,
        )(parts, w_out)
    parts = exchange(parts.reshape(groups, 8, width_local), "head")
    with jax.named_scope("deliver"):
        sent = call(
            deliver_kernel, jax.ShapeDtypeStruct((n_steps, width_total), BF16), [smem, vmem]
        )(owners, parts.reshape(8 * groups, width_local))
    return exchange(sent, ctx, 1)[None]


def solution(mesh):
    ctx = ("z", "xc")
    near = 8
    split = Mesh(
        mesh.devices.reshape(mesh.shape["ctx"] // near, near, mesh.shape["head"]),
        ("z", "xc", "head"),
    )
    placed = (
        P(None, None, ctx),
        P(ctx),
        P(ctx, "head"),
        P(ctx, "head"),
        P("head", ctx),
        P(ctx, None, "head", None),
        P(),
        P(),
        P(),
    )
    return jax.shard_map(
        body, mesh=split, in_specs=placed, out_specs=P(ctx, None, None), check_vma=False
    )
```

time: 107 us -> 102 us (0.953)
  blocking collectives: 57.4 us -> 68.5 us
  waiting for transfers between devices: 17.3 us -> 7.33 us
  starting transfers between devices: 19.5 us -> 14.8 us
  local copies, waits for them, and re-layouts: 5.77 us -> 2.97 us
  Pallas kernels: 4.11 us -> 6.66 us
  other arithmetic: 2.42 us -> 1.29 us
    all_to_all x4 -> x5, blocking collectives: 57.4 us -> 68.5 us  [exchange(): return lax.all_to_all(x, axis, dim, dim, tiled=True)]
    all_to_all x2 -> x1, waiting for transfers between devices: 17.3 us -> 7.33 us  [exchange(): return lax.all_to_all(x, axis, dim, dim, tiled=True)]
    all_to_all x2 -> x1, starting transfers between devices: 19.5 us -> 14.8 us  [exchange(): return lax.all_to_all(x, axis, dim, dim, tiled=True)]
    unnamed x12 -> x17, local copies, waits for them, and re-layouts: 2.83 us -> 0.68 us
    pallas_call x3, Pallas kernels: 1.72 us -> 3.86 us  [the longest x1 2.47 us: body(): call(project_kernel, jax.ShapeDtypeStruct((4 * peers, HD), F32), [hbm] *...]
    slice x0 -> x1, local copies, waits for them, and re-layouts: none -> 1.7 us  [body(): keys, values = (tokens[:, :HD], tokens[:, HD:])]
    reshape x3 -> x0, local copies, waits for them, and re-layouts: 1.49 us -> none  [the longest x1 0.81 us: body(): norm_gain.reshape(1, width_local)]
  transfers between devices with their start and end apart: 2 -> 1, of which waited for: 2 -> 1; matrix products, arithmetic and copies ran while one was open for 4% -> 4% of each run, Pallas kernels for 0% -> 0%
where the time goes in v2:
time: 102 us
  blocking collectives  68.5 us (67%)
  starting transfers between devices  14.8 us (15%)
  waiting for transfers between devices  7.33 us (7%)
  Pallas kernels  6.66 us (7%)
  local copies, waits for them, and re-layouts  2.97 us (3%)
  other arithmetic  1.29 us (1%)
    all_to_all x5, blocking collectives, exchange(): return lax.all_to_all(x, axis, dim, dim, tiled=True)  68.5 us
    all_to_all x1, starting transfers between devices, exchange(): return lax.all_to_all(x, axis, dim, dim, tiled=True)  14.8 us
    all_to_all x1, waiting for transfers between devices, exchange(): return lax.all_to_all(x, axis, dim, dim, tiled=True)  7.33 us
    pallas_call x1, Pallas kernels, body(): call(project_kernel, jax.ShapeDtypeStruct((4 * peers, HD), F32), [hbm] *...  2.47 us
  transfers between devices with their start and end apart: 1, of which 1 were waited for; matrix products, arithmetic and copies ran while one was open for 4% of the time, Pallas kernels for 0%

profile of v2, /device:TPU:1, one launch (start us, length us, event | category | flops | bytes accessed | tf_op | source)
XLA Modules:
  0.0 101.8 jit_solution(8958304259056908110)
XLA Ops:
  0.0 2.5 %project.1 = f32[256,128]{1,0:T(8,128)} custom-call(bf16[2,4,256]{2,1,0:T(4,128)(2,1)} %hidden_hbm.1, bf16[256]{0:T(256)(128)(2,1)} %gain_hbm.1, bf16[256,2048]{1,0:T(8,128)(2,1)} %wq_hbm.1, bf16[256,256]{1,0:T(8,128)(2,1)} %wkv_hbm.1), custom_call_target="tpu_custom_call" | custom-call | tf_op jit(solution)/shard_map/project/pallas_call | solution.py:272
  2.5 14.8 %all-to-all-start = ((f32[64,4,128]{2,1,0:T(4,128)}), f32[64,4,128]{2,1,0:T(4,128)S(1)}, u32[]{:S(2)}, u32[]{:S(2)}) async-start(f32[64,4,128]{2,1,0:T(4,128)} %bitcast.25), calls=%async_computation | async-start | bytes 262144 | tf_op jit(solution)/shard_map/all_to_all | solution.py:268
  17.4 0.0 copy-start.7
  17.4 0.0 copy-start.6
  17.4 0.0 copy-start.5
  17.4 0.0 copy-start.2
  17.4 0.0 copy-start.3
  17.5 0.0 copy-start.4
  17.5 1.7 %fusion.14 = (bf16[4096,128]{1,0:T(8,128)(2,1)S(1)}, bf16[4096,128]{1,0:T(8,128)(2,1)S(1)}) fusion(bf16[4096,256]{1,0:T(8,128)(2,1)} %bitcast.24), kind=kLoop, calls=%fused_computation.27 | loop fusion | bytes 4194304 | tf_op jit(solution)/shard_map/slice | solution.py:316
  19.2 0.0 copy-done.7
  19.2 0.0 copy-done.6
  19.2 0.0 copy-done.5
  19.2 0.1 subtract_clamp_fusion
  19.3 0.0 copy-done.2
  19.3 0.3 select_reduce_fusion
  19.7 0.1 fusion.12.first_ref
  19.8 0.6 dynamic_slice.3
  20.4 0.0 copy-done.3
  20.4 0.0 copy-done.4
  20.4 0.8 fusion.11
  21.1 7.3 %all-to-all-done = f32[64,4,128]{2,1,0:T(4,128)S(1)} async-done(((f32[64,4,128]{2,1,0:T(4,128)}), f32[64,4,128]{2,1,0:T(4,128)S(1)}, u32[]{:S(2)}, u32[]{:S(2)}) %all-to-all-start) | async-done | bytes 131104 | tf_op jit(solution)/shard_map/all_to_all | solution.py:268
  28.5 0.2 finish.1
  28.7 13.9 %all_to_all.34 = bf16[64,4,128]{2,1,0:T(4,128)(2,1)S(1)} all-to-all(bf16[64,4,128]{2,1,0:T(4,128)(2,1)S(1)} %bitcast.19), channel_id=1, replica_groups=mesh['z'=8,'xc'=8,'head'=8] {'z','xc'}, dimensions={0} | all-to-all | bytes 131072 | tf_op jit(solution)/shard_map/all_to_all | solution.py:268
  42.6 0.0 copy-start
  42.6 1.6 %attend.1 = bf16[1152,128]{1,0:T(8,128)(2,1)S(1)} custom-call(bf16[256,128]{1,0:T(8,128)(2,1)S(1)} %bitcast.20, s32[8,128]{1,0:T(8,128)S(1)} %pad_add_fusion.limit_ref, bf16[4096,128]{1,0:T(8,128)(2,1)S(1)} %get-tuple-element.25.keys_ref, bf16[4096,128]{1,0:T(8,128)(2,1)S(1)} %get-tuple-element.26.values_ref), custom_call_target="tpu_custom_call" | custom-call | tf_op jit(solution)/shard_map/attend/pallas_call | solution.py:330
  44.2 0.0 copy-start.1
  44.2 10.1 %all_to_all.35 = bf16[8,144,128]{2,1,0:T(8,128)(2,1)S(1)} all-to-all(bf16[8,144,128]{2,1,0:T(8,128)(2,1)S(1)} %bitcast.14), channel_id=1, replica_groups=mesh['z'=8,'xc'=8,'head'=8] {'xc'}, dimensions={0} | all-to-all | bytes 589824 | tf_op jit(solution)/shard_map/all_to_all | solution.py:268
  54.3 0.8 merge.1
  55.1 14.7 %all_to_all.36 = bf16[8,144,128]{2,1,0:T(8,128)(2,1)S(1)} all-to-all(bf16[8,144,128]{2,1,0:T(8,128)(2,1)S(1)} %bitcast.16), channel_id=1, replica_groups=mesh['z'=8,'xc'=8,'head'=8] {'z'}, dimensions={0} | all-to-all | bytes 589824 | tf_op jit(solution)/shard_map/all_to_all | solution.py:268
  69.8 0.0 copy-done
  69.8 1.0 output.1
  70.8 13.8 %all_to_all.37 = f32[8,8,256]{2,1,0:T(8,128)S(1)} all-to-all(f32[8,8,256]{2,1,0:T(8,128)S(1)} %bitcast.21), channel_id=1, replica_groups=mesh['z'=8,'xc'=8,'head'=8] {'head'}, dimensions={0} | all-to-all | bytes 131072 | tf_op jit(solution)/shard_map/all_to_all | solution.py:268
  84.6 0.0 copy-done.1
  84.6 0.6 deliver.1
  85.2 16.0 %all_to_all.38 = bf16[2,64,256]{2,0,1:T(2,128)(2,1)S(1)} all-to-all(bf16[2,64,256]{2,0,1:T(2,128)(2,1)S(1)} %bitcast.23), channel_id=1, replica_groups=mesh['z'=8,'xc'=8,'head'=8] {'z','xc'}, dimensions={1} | all-to-all | bytes 131072 | tf_op jit(solution)/shard_map/all_to_all | solution.py:268
  101.2 0.6 copy.19
  (7 shorter events, 0.0 us)
Async XLA Ops:
  2.5 26.0 %all-to-all-start = ((f32[64,4,128]{2,1,0:T(4,128)}), f32[64,4,128]{2,1,0:T(4,128)S(1)}, u32[]{:S(2)}, u32[]{:S(2)}) async-start(f32[64,4,128]{2,1,0:T(4,128)} %bitcast.25), calls=%async_computation | async-start | bytes 262144 | tf_op jit(solution)/shard_map/all_to_all | solution.py:268
  17.4 1.8 %copy-start.7 = (pred[128]{0:T(512)(128)(4,1)S(1)}, pred[128]{0:T(512)(128)(4,1)}, u32[]{:S(2)}) copy-start(pred[128]{0:T(512)(128)(4,1)} %constant.67.clone) | copy-start | bytes 388
  17.4 1.8 %copy-start.6 = (pred[128]{0:T(512)(128)(4,1)S(1)}, pred[128]{0:T(512)(128)(4,1)}, u32[]{:S(2)}) copy-start(pred[128]{0:T(512)(128)(4,1)} %constant.65.clone) | copy-start | bytes 388
  17.4 1.8 %copy-start.5 = (s32[4]{0:T(128)S(1)}, s32[4]{0:T(128)}, u32[]{:S(2)}) copy-start(s32[4]{0:T(128)} %param.22) | copy-start | bytes 52
  17.4 1.9 %copy-start.2 = (s32[4,256]{1,0:T(4,128)S(1)}, s32[4,256]{1,0:T(4,128)}, u32[]{:S(2)}) copy-start(s32[4,256]{1,0:T(4,128)} %param.21) | copy-start | bytes 12292
  17.4 2.9 %copy-start.3 = (f32[128]{0:T(128)S(1)}, f32[128]{0:T(128)}, u32[]{:S(2)}) copy-start(f32[128]{0:T(128)} %constant.70) | copy-start | bytes 1540
  17.5 2.9 %copy-start.4 = (f32[128]{0:T(128)S(1)}, f32[128]{0:T(128)}, u32[]{:S(2)}) copy-start(f32[128]{0:T(128)} %constant.69) | copy-start | bytes 1540
  42.6 27.3 %copy-start = (bf16[2048,256]{1,0:T(8,128)(2,1)S(1)}, bf16[2048,256]{1,0:T(8,128)(2,1)}, u32[]{:S(2)}) copy-start(bf16[2048,256]{1,0:T(8,128)(2,1)} %w_ref.1) | copy-start | bytes 3145732
  44.2 40.5 %copy-start.1 = (s32[4]{0:T(128)S(1)}, s32[4]{0:T(128)}, u32[]{:S(2)}) copy-start(s32[4]{0:T(128)} %owners_ref.1) | copy-start | bytes 52

commit v3 on v2

--- a/solution.py
+++ b/solution.py
@@ -19,15 +19,14 @@
 
 
 def frequencies(head_size):
-    index = np.arange(head_size // 2)
-    inverse = 500000.0 ** (-2.0 * index / head_size)
+    halfway = head_size // 2
+    inverse = 500000.0 ** (-(jnp.arange(halfway, dtype=F32) * 2.0 / head_size))
     wavelength = 2.0 * math.pi / inverse
     smooth = (8192.0 / wavelength - 1.0) / 3.0
     blended = (1.0 - smooth) * inverse / 8.0 + smooth * inverse
-    chosen = np.where(
-        wavelength < 2048.0, inverse, np.where(wavelength > 8192.0, inverse / 8.0, blended)
-    )
-    return chosen.astype(np.float32)
+    return jnp.where(
+        wavelength < 2048.0, inverse, jnp.where(wavelength > 8192.0, inverse / 8.0, blended)
+    )
 
 
 def iota(shape, dim):
@@ -63,6 +62,56 @@
     rest = x - first
     second = rest.astype(BF16).astype(F32)
     return first, second, rest - second
+
+
+TILE = 16
+CODE = math.log(2.0) / 128.0
+TOP = 32000.0
+
+
+def encode(heads, rest, out_ref):
+    scales, marks = [], []
+    lane = iota((8, HD), 1)
+    largest = jnp.abs(heads[0])
+    for x in heads[1:]:
+        largest = jnp.maximum(largest, jnp.abs(x))
+    mark = jnp.zeros((8, HD), F32)
+    for k, x in enumerate([largest] + [jnp.abs(x) for x in rest]):
+        most = jnp.maximum(jnp.max(x, axis=-1, keepdims=True), 1e-28)
+        exponent = jnp.ceil(jnp.log(most * (1.0 / TOP)) * (1.0 / CODE))
+        scales.append(jnp.exp(exponent * -CODE))
+        mark = jnp.where(lane // (HD // 4) == k, exponent, mark)
+    tiles = [x * scales[0] for x in heads] + [x * s for x, s in zip(rest, scales[1:])] + [mark]
+    pairs = [
+        jnp.round(jnp.concatenate(tiles[k : k + 2], axis=0)).astype(jnp.int32).astype(jnp.int16)
+        for k in range(0, len(tiles), 2)
+    ]
+    block = TILE * len(pairs)
+    for n in range(out_ref.shape[0] // block):
+        for k, pair in enumerate(pairs):
+            start = n * block + k * TILE
+            out_ref[start : start + TILE, :] = pair
+
+
+def decode(parts_ref, heads):
+    pairs = heads // 2 + 2
+    block = TILE * pairs
+    sums = None
+    for n in range(parts_ref.shape[0] // block):
+        tiles = [
+            parts_ref[n * block + k * TILE : n * block + (k + 1) * TILE, :]
+            .astype(jnp.int32)
+            .astype(F32)
+            for k in range(pairs)
+        ]
+        scale = jnp.exp(tiles[-1][8:16] * CODE)
+        cols = [scale[:, k * (HD // 4) : k * (HD // 4) + 1] for k in range(4)]
+        twice = jnp.concatenate([cols[0], cols[0]], axis=0)
+        terms = [x * twice for x in tiles[:-2]]
+        terms += [tiles[-2][0:8] * cols[1], tiles[-2][8:16] * cols[2], tiles[-1][0:8] * cols[3]]
+        sums = terms if sums is None else [x + y for x, y in zip(sums, terms)]
+    queries = [x[8 * k : 8 * k + 8] for x in sums[:-3] for k in range(2)]
+    return queries, sums[-3:]
 
 
 def project_kernel(
@@ -85,77 +134,69 @@
     copies[0].wait()
     copies[1].wait()
     gain = gain_ref[...].astype(F32).reshape(1, gain_ref.shape[0])
-    hid = [hidden_ref[s].astype(F32) for s in range(2)]
-    width = hid[0].shape[1]
-    row = iota((16, width), 0) % 4
-    spread = [
-        jnp.concatenate([h[b : b + 1] for b in range(4) for _ in range(4)], axis=0) for h in hid
-    ]
-    scaled = [x * gain for x in spread]
-    zero = jnp.zeros_like(scaled[0])
-    lhs_q = split2(jnp.where(row == 0, scaled[0], jnp.where(row == 1, scaled[1], zero)))
-    lhs_q = jnp.concatenate(lhs_q, axis=0)
-    lhs_kv = [split2(jnp.where(row == 2, x, zero)) for x in scaled]
-    lhs_kv = jnp.concatenate([p for pair in lhs_kv for p in pair], axis=0)
-    squares = [jnp.sum(x * x, axis=-1, keepdims=True) for x in spread]
-    square = jnp.where(iota((16, HD), 1) < HALF, squares[0], squares[1])
-    square = jnp.where(iota((16, HD), 0) % 4 == 3, square, 0.0)
+    hid = jnp.concatenate([hidden_ref[s].astype(F32) for s in range(2)], axis=0)
+    lhs = jnp.concatenate(split2(hid * gain), axis=0)
+    square = jnp.broadcast_to(jnp.sum(hid * hid, axis=-1, keepdims=True), (8, HD))
     copies[2].wait()
-    part_kv = dot(lhs_kv, wkv_ref[...])
-    part_kv = [part_kv[0:16] + part_kv[16:32], part_kv[32:48] + part_kv[48:64]]
+    part = dot(lhs, wkv_ref[...])
+    part = part[0:8] + part[8:16]
+    rest = [part[:, :HD], part[:, HD:], square]
+    heads = []
     for k in range(chunks):
         copies[3 + k].wait()
-        part_q = dot(lhs_q, wq_ref[:, k * chunk : (k + 1) * chunk])
-        part_q = part_q[0:16] + part_q[16:32]
-        for g in range(chunk // HD):
-            h = k * (chunk // HD) + g
-            block = part_q[:, g * HD : (g + 1) * HD] + square
-            if h < 4:
-                block = block + part_kv[h % 2][:, (h // 2) * HD : (h // 2 + 1) * HD]
-            out_ref[h * 16 : (h + 1) * 16, :] = block
-
-
-def finish_kernel(inverse_width, parts_ref, cos_ref, sin_ref, first_ref, out_ref):
-    n = parts_ref.shape[0]
-    total = parts_ref[0:8, :]
-    for k in range(1, n // 8):
-        total = total + parts_ref[k * 8 : (k + 1) * 8, :]
-    total = total + pltpu.roll(total, 4, 0)
-    root = lax.rsqrt(total * inverse_width + EPSILON)
-    root0 = root[3:4, 0:1]
-    root1 = root[3:4, HALF : HALF + 1]
-    scaled = total * jnp.where(first_ref[...] > 0.5, root0, root1)
-    turned = scaled * cos_ref[...] + pltpu.roll(scaled, HALF, 1) * sin_ref[...]
-    twice = jnp.concatenate([turned, turned], axis=0).astype(BF16)
-    for k in range(n // 16):
-        out_ref[k * 16 : (k + 1) * 16, :] = twice
-
-
-def attend_kernel(scale, rows_ref, limit_ref, keys_ref, values_ref, out_ref, flat_ref, score_ref):
-    flat_ref[...] = rows_ref[...].astype(F32)
-    peers = flat_ref.shape[0] // 4
-    rows = 2 * peers
-    query = jnp.concatenate(
-        [flat_ref[pl.ds(i, peers, stride=4), :] for i in range(2)], axis=0
-    ).astype(BF16)
-    new = flat_ref[pl.ds(2, 16, stride=4), :]
-    new_keys = new.astype(BF16)
-    new_values = pltpu.roll(new, 8, 0).astype(BF16)
+        part = dot(lhs, wq_ref[:, k * chunk : (k + 1) * chunk])
+        part = part[0:8] + part[8:16]
+        heads += [part[:, g * HD : (g + 1) * HD] for g in range(chunk // HD)]
+    encode(heads, rest, out_ref)
+
+
+def sum_kernel(heads, parts_ref, out_ref):
+    encode(*decode(parts_ref, heads), out_ref)
+
+
+def attend_kernel(
+    scale, inverse_width, parts_ref, cos_ref, sin_ref, limit_ref, keys_ref, values_ref, out_ref,
+    score_ref,
+):
+    rows = HD
+    queries, (key, value, square) = decode(parts_ref, rows // 8)
+    root = lax.rsqrt(square * inverse_width + EPSILON)
+
+    def turn(x):
+        x = x * root
+        return x * cos_ref[...] + pltpu.roll(x, HALF, 1) * sin_ref[...]
+
+    query = jnp.concatenate([turn(x) for x in queries], axis=0)
+    query = jnp.concatenate(split2(query), axis=0)
+    new_keys = turn(key)
+    new_values = value * root
+    new_keys, new_values = [
+        jnp.concatenate(pair, axis=0).astype(BF16)
+        for pair in ((new_keys, new_values), (new_values, new_keys))
+    ]
     tokens = keys_ref.shape[0]
     page = HD
     lane8 = iota((8, page), 1)
     chunk = 4 * page
 
-    row = iota((rows, 16), 0)
+    def score(keys):
+        both = dot_t(query, keys)
+        return (both[:rows] + both[rows:]) * scale
+
+    def mix(weights, values):
+        both = dot(jnp.concatenate(split2(weights), axis=0), values)
+        return both[:rows] + both[rows:]
+
+    row = iota((rows, 16), 0) % 8
     col = iota((rows, 16), 1)
-    new_ok = (
-        (col < 8) & (col % 4 == row % 4) & (col // 4 <= row // peers)
-    ) & (limit_ref[0:1, page - 1 : page] > 0)
-    new_scores = jnp.where(new_ok, dot_t(query, new_keys) * scale, NEGATIVE)
+    new_ok = ((col < 8) & (col % 4 == row % 4) & (col // 4 <= row // 4)) & (
+        limit_ref[0:1, page - 1 : page] > 0
+    )
+    new_scores = jnp.where(new_ok, score(new_keys), NEGATIVE)
 
     best = None
     for start in range(0, tokens, chunk):
-        part = dot_t(query, keys_ref[start : start + chunk, :]) * scale
+        part = score(keys_ref[start : start + chunk, :])
         for k in range(chunk // page):
             p = start // page + k
             ok = lane8 < limit_ref[:, p : p + 1]
@@ -169,15 +210,13 @@
     top = jnp.maximum(top, FLOOR)
     new_weights = jnp.exp(new_scores - top)
     total = jnp.sum(new_weights, axis=-1, keepdims=True)
-    mixed = dot(new_weights.astype(BF16), new_values)
+    mixed = mix(new_weights, new_values)
     sums = jnp.zeros((rows, page), F32)
     for start in range(0, tokens, chunk):
         weights = jnp.exp(score_ref[:, start : start + chunk] - top)
         for k in range(chunk // page):
             sums = sums + weights[:, k * page : (k + 1) * page]
-        pair = jnp.concatenate(split2(weights), axis=0)
-        pair = dot(pair, values_ref[start : start + chunk, :])
-        mixed = mixed + pair[:rows] + pair[rows:]
+        mixed = mixed + mix(weights, values_ref[start : start + chunk, :])
     total = total + jnp.sum(sums, axis=-1, keepdims=True)
     post(mixed, top, total, out_ref)
 
@@ -228,15 +267,10 @@
 def output_kernel(parts_ref, w_ref, out_ref):
     mixed, _, total = merge(parts_ref)
     rows = mixed / total
-    half = rows.shape[0] // 2
-    lhs = jnp.concatenate(
-        [
-            jnp.concatenate([rows[i * half + h * 4 : i * half + h * 4 + 4] for i in range(2)], axis=0)
-            for h in range(half // 4)
-        ],
-        axis=1,
-    )
-    part = dot(lhs.astype(BF16), w_ref[...])
+    heads = rows.shape[0] // 8
+    lhs = jnp.concatenate([rows[h * 8 : h * 8 + 8] for h in range(heads)], axis=1)
+    part = dot(jnp.concatenate(split2(lhs), axis=0), w_ref[...])
+    part = part[0:8] + part[8:16]
     for k in range(out_ref.shape[0] // 8):
         out_ref[k * 8 : (k + 1) * 8, :] = part
 
@@ -267,11 +301,15 @@
     def exchange(x, axis, dim=0):
         return lax.all_to_all(x, axis, dim, dim, tiled=True)
 
+    heads = w_query.shape[1] // HD
+    coded = TILE * (heads // 2 + 2)
+    block = 8 * heads + STATS
+
     with jax.named_scope("project"):
         chunks = 4
         parts = call(
             project_kernel,
-            jax.ShapeDtypeStruct((4 * peers, HD), F32),
+            jax.ShapeDtypeStruct((near * coded, HD), jnp.int16),
             [hbm] * 4,
             scratch=[
                 pltpu.VMEM(hidden.shape, BF16),
@@ -285,22 +323,13 @@
     parts, lengths, page_table, cache = lax.optimization_barrier(
         (parts, lengths, page_table, cache)
     )
-    parts = exchange(parts.reshape(peers, 4, HD), ctx).reshape(4 * peers, HD)
-
-    request = lax.rem(device_now, n_reqs)
-    head = lax.div(device_now, n_reqs)
-    kv_step = lax.rem(head, 2)
-    row = lax.broadcasted_iota(jnp.int32, (8, HD), 0) % 4
-    steps = jnp.where(row == 1, 1, jnp.where(row == 2, kv_step, 0))
-    turns = (row < 2) | ((row == 2) & (head < 2))
-    near_length = lax.dynamic_slice(lengths, (request,), (1,))[0]
-    position = (near_length + steps).astype(F32)
-    freq = np.concatenate([frequencies(HD)] * 2)
-    sign = np.concatenate([-np.ones(HALF, np.float32), np.ones(HALF, np.float32)])
-    angles = position * freq[None, :]
-    cosine = jnp.where(turns, jnp.cos(angles), 1.0)
-    sine = jnp.where(turns, jnp.sin(angles) * sign[None, :], 0.0)
-    first = (steps == 0).astype(F32)
+    parts = exchange(parts.reshape(near, coded, HD), "xc").reshape(near * coded, HD)
+
+    position = (lengths[None, :] + jnp.arange(n_steps, dtype=jnp.int32)[:, None]).astype(F32)
+    angles = position.reshape(n_steps * n_reqs, 1) * frequencies(HD)
+    cosine, sine = jnp.cos(angles), jnp.sin(angles)
+    cosine = jnp.concatenate([cosine, cosine], axis=-1)
+    sine = jnp.concatenate([-sine, sine], axis=-1)
 
     lane = np.arange(HD, dtype=np.int32)
     global_ids = jnp.where(lane < pages, device_now * pages + lane, -2)
@@ -314,28 +343,24 @@
     limit = jnp.concatenate([limit, limit], axis=0)
     tokens = cache.reshape(pages * page_len, 2 * HD)
     keys, values = tokens[:, :HD], tokens[:, HD:]
-    parts, cosine, sine, first, limit, keys, values = lax.optimization_barrier(
-        (parts, cosine, sine, first, limit, keys, values)
-    )
-
-    with jax.named_scope("finish"):
-        rows = call(
-            functools.partial(finish_kernel, 1.0 / width_total),
-            jax.ShapeDtypeStruct((4 * peers, HD), BF16),
-            [vmem] * 4,
-        )(parts, cosine, sine, first)
-    rows = exchange(rows.reshape(peers, 4, HD), ctx).reshape(4 * peers, HD)
-    block = 2 * peers + STATS
+    parts, cosine, sine, limit, keys, values = lax.optimization_barrier(
+        (parts, cosine, sine, limit, keys, values)
+    )
+
+    with jax.named_scope("sum"):
+        parts = call(
+            functools.partial(sum_kernel, heads),
+            jax.ShapeDtypeStruct((far * coded, HD), jnp.int16),
+            [vmem],
+        )(parts)
+    parts = exchange(parts.reshape(far, coded, HD), "z").reshape(far * coded, HD)
     with jax.named_scope("attend"):
         parts = call(
-            functools.partial(attend_kernel, HD ** (-0.5)),
+            functools.partial(attend_kernel, HD ** (-0.5), 1.0 / width_total),
             jax.ShapeDtypeStruct((near * block, HD), BF16),
-            [vmem] * 4,
-            scratch=[
-                pltpu.VMEM((4 * peers, HD), F32),
-                pltpu.VMEM((2 * peers, pages * page_len), F32),
-            ],
-        )(rows, limit, keys, values)
+            [vmem] * 6,
+            scratch=[pltpu.VMEM((8 * heads, pages * page_len), F32)],
+        )(parts, cosine, sine, limit, keys, values)
     parts = exchange(parts.reshape(near, block, HD), "xc").reshape(near * block, HD)
     with jax.named_scope("merge"):
         parts = call(

time: 102 us -> 99.7 us (0.977)
  blocking collectives: 68.5 us -> 73.9 us
  starting transfers between devices: 14.8 us -> 10.2 us
  waiting for transfers between devices: 7.33 us -> 4.63 us
    all_to_all x5, blocking collectives: 68.5 us -> 73.9 us  [exchange(): return lax.all_to_all(x, axis, dim, dim, tiled=True)]
    all_to_all x1, starting transfers between devices: 14.8 us -> 10.2 us  [exchange(): return lax.all_to_all(x, axis, dim, dim, tiled=True)]
    all_to_all x1, waiting for transfers between devices: 7.33 us -> 4.63 us  [exchange(): return lax.all_to_all(x, axis, dim, dim, tiled=True)]
  transfers between devices with their start and end apart: 1 -> 1, of which waited for: 1 -> 1; matrix products, arithmetic and copies ran while one was open for 4% -> 2% of each run, Pallas kernels for 0% -> 0%
where the time goes in v3:
time: 99.7 us; the launch traced here: 99.3 us
  blocking collectives  73.9 us (74%)
  starting transfers between devices  10.2 us (10%)
  Pallas kernels  7.38 us (7%)
  waiting for transfers between devices  4.63 us (5%)
  local copies, waits for them, and re-layouts  2.42 us (2%)
    all_to_all x5, blocking collectives, exchange(): return lax.all_to_all(x, axis, dim, dim, tiled=True)  73.9 us
    all_to_all x1, starting transfers between devices, exchange(): return lax.all_to_all(x, axis, dim, dim, tiled=True)  10.2 us
    all_to_all x1, waiting for transfers between devices, exchange(): return lax.all_to_all(x, axis, dim, dim, tiled=True)  4.63 us
    pallas_call x1, Pallas kernels, body(): call(project_kernel, jax.ShapeDtypeStruct((near * coded, HD), jnp.int16),...  2.65 us
    pallas_call x1, Pallas kernels, body(): call(functools.partial(attend_kernel, HD ** (-0.5), 1.0 / width_total), j...  2.1 us
  transfers between devices with their start and end apart: 1, of which 1 were waited for; matrix products, arithmetic and copies ran while one was open for 2% of the time, Pallas kernels for 0%

profile of v3, /device:TPU:1, one launch (start us, length us, event | category | flops | bytes accessed | tf_op | source)
XLA Modules:
  0.0 99.3 jit_solution(10419503502464370937)
XLA Ops:
  0.0 0.0 copy-start.5
  0.0 0.0 copy-start.4
  0.0 0.0 copy-start.3
  0.0 0.0 copy-start.2
  0.0 2.7 %project.1 = s16[1280,128]{1,0:T(8,128)(2,1)} custom-call(bf16[2,4,256]{2,1,0:T(4,128)(2,1)} %hidden_hbm.1, bf16[256]{0:T(256)(128)(2,1)} %gain_hbm.1, bf16[256,2048]{1,0:T(8,128)(2,1)} %wq_hbm.1, bf16[256,256]{1,0:T(8,128)(2,1)} %wkv_hbm.1), custom_call_target="tpu_custom_call" | custom-call | tf_op jit(solution)/shard_map/project/pallas_call | solution.py:310
  2.7 10.2 %all-to-all-start = ((s16[8,160,128]{2,1,0:T(8,128)(2,1)}), s16[8,160,128]{2,1,0:T(8,128)(2,1)S(1)}, u32[]{:S(2)}, u32[]{:S(2)}) async-start(s16[8,160,128]{2,1,0:T(8,128)(2,1)} %bitcast.24), calls=%async_computation | async-start | bytes 655360 | tf_op jit(solution)/shard_map/all_to_all | solution.py:302
  12.9 0.0 copy-done.3
  13.0 0.1 convert_element_type.14
  13.0 0.1 subtract_clamp_fusion
  13.1 0.0 copy-done.5
  13.1 0.0 copy-done.4
  13.2 0.0 copy-done.2
  13.2 0.3 select_reduce_fusion
  13.5 1.7 %fusion.1 = (bf16[4096,128]{1,0:T(8,128)(2,1)S(1)}, bf16[4096,128]{1,0:T(8,128)(2,1)S(1)}) fusion(bf16[4096,256]{1,0:T(8,128)(2,1)} %bitcast.23), kind=kLoop, calls=%fused_computation.15 | loop fusion | bytes 4194304 | tf_op jit(solution)/shard_map/slice | solution.py:345
  15.2 0.1 fusion
  15.3 0.1 pad_maximum_fusion
  15.4 4.6 %all-to-all-done = s16[8,160,128]{2,1,0:T(8,128)(2,1)S(1)} async-done(((s16[8,160,128]{2,1,0:T(8,128)(2,1)}), s16[8,160,128]{2,1,0:T(8,128)(2,1)S(1)}, u32[]{:S(2)}, u32[]{:S(2)}) %all-to-all-start) | async-done | bytes 327712 | tf_op jit(solution)/shard_map/all_to_all | solution.py:302
  20.0 0.3 sum.1
  20.3 16.5 %all_to_all.34 = s16[8,160,128]{2,1,0:T(8,128)(2,1)S(1)} all-to-all(s16[8,160,128]{2,1,0:T(8,128)(2,1)S(1)} %bitcast.14), channel_id=1, replica_groups=mesh['z'=8,'xc'=8,'head'=8] {'z'}, dimensions={0} | all-to-all | bytes 655360 | tf_op jit(solution)/shard_map/all_to_all | solution.py:302
  36.8 0.0 copy-start
  36.8 2.1 %attend.1 = bf16[1152,128]{1,0:T(8,128)(2,1)S(1)} custom-call(s16[1280,128]{1,0:T(8,128)(2,1)S(1)} %bitcast.15, f32[8,128]{1,0:T(8,128)S(1)} %get-tuple-element.20.cos_ref, f32[8,128]{1,0:T(8,128)S(1)} %get-tuple-element.21.sin_ref, s32[8,128]{1,0:T(8,128)S(1)} %pad_add_fusion.limit_ref, bf16[4096,128]{1,0:T(8,128)(2,1)S(1)} %get-tuple-element.23.keys_ref, ...), custom_call_target="tpu_custom_call" | custom-call | tf_op jit(solution)/shard_map/attend/pallas_call | solution.py:358
  38.9 0.0 copy-start.1
  38.9 12.9 %all_to_all.35 = bf16[8,144,128]{2,1,0:T(8,128)(2,1)S(1)} all-to-all(bf16[8,144,128]{2,1,0:T(8,128)(2,1)S(1)} %bitcast.18), channel_id=1, replica_groups=mesh['z'=8,'xc'=8,'head'=8] {'xc'}, dimensions={0} | all-to-all | bytes 589824 | tf_op jit(solution)/shard_map/all_to_all | solution.py:302
  51.8 0.8 merge.1
  52.6 14.7 %all_to_all.36 = bf16[8,144,128]{2,1,0:T(8,128)(2,1)S(1)} all-to-all(bf16[8,144,128]{2,1,0:T(8,128)(2,1)S(1)} %bitcast.17), channel_id=1, replica_groups=mesh['z'=8,'xc'=8,'head'=8] {'z'}, dimensions={0} | all-to-all | bytes 589824 | tf_op jit(solution)/shard_map/all_to_all | solution.py:302
  67.3 0.0 copy-done
  67.3 1.0 output.1
  68.3 13.8 %all_to_all.37 = f32[8,8,256]{2,1,0:T(8,128)S(1)} all-to-all(f32[8,8,256]{2,1,0:T(8,128)S(1)} %bitcast.20), channel_id=1, replica_groups=mesh['z'=8,'xc'=8,'head'=8] {'head'}, dimensions={0} | all-to-all | bytes 131072 | tf_op jit(solution)/shard_map/all_to_all | solution.py:302
  82.2 0.0 copy-done.1
  82.2 0.6 deliver.1
  82.7 16.0 %all_to_all.38 = bf16[2,64,256]{2,0,1:T(2,128)(2,1)S(1)} all-to-all(bf16[2,64,256]{2,0,1:T(2,128)(2,1)S(1)} %bitcast.22), channel_id=1, replica_groups=mesh['z'=8,'xc'=8,'head'=8] {'z','xc'}, dimensions={1} | all-to-all | bytes 131072 | tf_op jit(solution)/shard_map/all_to_all | solution.py:302
  98.7 0.6 copy.17
  (7 shorter events, 0.1 us)
Async XLA Ops:
  0.0 13.1 %copy-start.5 = (pred[128]{0:T(512)(128)(4,1)S(1)}, pred[128]{0:T(512)(128)(4,1)}, u32[]{:S(2)}) copy-start(pred[128]{0:T(512)(128)(4,1)} %constant.53.clone) | copy-start | bytes 388
  0.0 13.1 %copy-start.4 = (pred[128]{0:T(512)(128)(4,1)S(1)}, pred[128]{0:T(512)(128)(4,1)}, u32[]{:S(2)}) copy-start(pred[128]{0:T(512)(128)(4,1)} %constant.51.clone) | copy-start | bytes 388
  0.0 12.9 %copy-start.3 = (s32[4]{0:T(128)S(1)}, s32[4]{0:T(128)}, u32[]{:S(2)}) copy-start(s32[4]{0:T(128)} %param.20) | copy-start | bytes 52
  0.0 13.1 %copy-start.2 = (s32[4,256]{1,0:T(4,128)S(1)}, s32[4,256]{1,0:T(4,128)}, u32[]{:S(2)}) copy-start(s32[4,256]{1,0:T(4,128)} %param.19) | copy-start | bytes 12292
  2.7 17.4 %all-to-all-start = ((s16[8,160,128]{2,1,0:T(8,128)(2,1)}), s16[8,160,128]{2,1,0:T(8,128)(2,1)S(1)}, u32[]{:S(2)}, u32[]{:S(2)}) async-start(s16[8,160,128]{2,1,0:T(8,128)(2,1)} %bitcast.24), calls=%async_computation | async-start | bytes 655360 | tf_op jit(solution)/shard_map/all_to_all | solution.py:302
  36.8 30.6 %copy-start = (bf16[2048,256]{1,0:T(8,128)(2,1)S(1)}, bf16[2048,256]{1,0:T(8,128)(2,1)}, u32[]{:S(2)}) copy-start(bf16[2048,256]{1,0:T(8,128)(2,1)} %w_ref.1) | copy-start | bytes 3145732
  38.9 43.3 %copy-start.1 = (s32[4]{0:T(128)S(1)}, s32[4]{0:T(128)}, u32[]{:S(2)}) copy-start(s32[4]{0:T(128)} %owners_ref.1) | copy-start | bytes 52

commit v4 on v3

--- a/solution.py
+++ b/solution.py
@@ -218,19 +218,27 @@
             sums = sums + weights[:, k * page : (k + 1) * page]
         mixed = mixed + mix(weights, values_ref[start : start + chunk, :])
     total = total + jnp.sum(sums, axis=-1, keepdims=True)
-    post(mixed, top, total, out_ref)
+    post(mixed, tiled(top), tiled(total), out_ref)
 
 
 STATS = 16
+GROUP = 16
+
+
+def tiled(columns):
+    lane = iota((8, HD), 1)
+    tile = jnp.zeros((8, HD), F32)
+    for h in range(columns.shape[0] // 8):
+        tile = jnp.where(lane == h, columns[8 * h : 8 * h + 8], tile)
+    return tile
 
 
 def post(mixed, top, total, out_ref):
     rows = mixed.shape[0]
-    lane = iota((rows, HD), 1)
-    stats = jnp.zeros((rows, HD), F32)
+    tile = jnp.zeros((8, HD), F32)
     for k, piece in enumerate(split3(top) + split3(total)):
-        stats = jnp.where(lane == k, piece, stats)
-    stats = jnp.transpose(stats)[0:STATS].astype(BF16)
+        tile = tile + (pltpu.roll(piece, k * GROUP, 1) if k else piece)
+    stats = jnp.concatenate([tile, jnp.zeros_like(tile)], axis=0).astype(BF16)
     mixed = mixed.astype(BF16)
     block = rows + STATS
     for k in range(out_ref.shape[0] // block):
@@ -242,33 +250,45 @@
     rows = HD
     block = rows + STATS
     peers = parts_ref.shape[0] // block
-    stats = jnp.concatenate(
-        [parts_ref[k * block + rows : (k + 1) * block, :].astype(F32) for k in range(peers)],
-        axis=0,
-    )
-    stats = jnp.transpose(stats)
-    stats = stats + pltpu.roll(stats, HD - 1, 1) + pltpu.roll(stats, HD - 2, 1)
-    leading = iota((rows, HD), 1) % STATS == 0
-    top = jnp.max(jnp.where(leading, stats, NEGATIVE), axis=-1, keepdims=True)
-    factor = jnp.where(leading, jnp.exp(jnp.where(leading, stats, top) - top), 0.0)
-    total = jnp.sum(factor * pltpu.roll(stats, HD - 3, 1), axis=-1, keepdims=True)
-    mixed = jnp.zeros((rows, HD), F32)
+    tops, totals = [], []
     for k in range(peers):
-        part = parts_ref[k * block : k * block + rows, :].astype(F32)
-        mixed = mixed + factor[:, k * STATS : k * STATS + 1] * part
+        tile = parts_ref[k * block + rows : (k + 1) * block, :].astype(F32)[0:8]
+        tile = tile + pltpu.roll(tile, HD - GROUP, 1) + pltpu.roll(tile, HD - 2 * GROUP, 1)
+        tops.append(tile)
+        totals.append(pltpu.roll(tile, HD - 3 * GROUP, 1))
+    top = functools.reduce(jnp.maximum, tops)
+    factors = [jnp.exp(x - top) for x in tops]
+    total = sum(f * t for f, t in zip(factors, totals))
+    mixed = []
+    for g in range(rows // 16):
+        acc = None
+        for k in range(peers):
+            part = parts_ref[k * block + 16 * g : k * block + 16 * g + 16, :].astype(F32)
+            f = factors[k]
+            f = jnp.concatenate([f[:, 2 * g : 2 * g + 1], f[:, 2 * g + 1 : 2 * g + 2]], axis=0)
+            acc = f * part if acc is None else acc + f * part
+        mixed.append(acc)
     return mixed, top, total
 
 
 def merge_kernel(parts_ref, out_ref):
     mixed, top, total = merge(parts_ref)
-    post(mixed, top, total, out_ref)
+    live = iota((8, HD), 1) < GROUP
+    post(
+        jnp.concatenate(mixed, axis=0), jnp.where(live, top, 0.0), jnp.where(live, total, 0.0), out_ref
+    )
 
 
 def output_kernel(parts_ref, w_ref, out_ref):
     mixed, _, total = merge(parts_ref)
-    rows = mixed / total
-    heads = rows.shape[0] // 8
-    lhs = jnp.concatenate([rows[h * 8 : h * 8 + 8] for h in range(heads)], axis=1)
+    inverse = 1.0 / jnp.where(iota((8, HD), 1) < GROUP, total, 1.0)
+    lhs = jnp.concatenate(
+        [
+            mixed[h // 2][8 * (h % 2) : 8 * (h % 2) + 8] * inverse[:, h : h + 1]
+            for h in range(2 * len(mixed))
+        ],
+        axis=1,
+    )
     part = dot(jnp.concatenate(split2(lhs), axis=0), w_ref[...])
     part = part[0:8] + part[8:16]
     for k in range(out_ref.shape[0] // 8):

time: 99.7 us -> 98.8 us (level)
  no operation moved by 1% of the time
where the time goes in v4:
time: 98.8 us; the launch traced here: 98.4 us
  blocking collectives  73.9 us (75%)
  starting transfers between devices  10.2 us (10%)
  Pallas kernels  6.42 us (6%)
  waiting for transfers between devices  4.63 us (5%)
  local copies, waits for them, and re-layouts  2.42 us (2%)
    all_to_all x5, blocking collectives, exchange(): return lax.all_to_all(x, axis, dim, dim, tiled=True)  73.9 us
    all_to_all x1, starting transfers between devices, exchange(): return lax.all_to_all(x, axis, dim, dim, tiled=True)  10.2 us
    all_to_all x1, waiting for transfers between devices, exchange(): return lax.all_to_all(x, axis, dim, dim, tiled=True)  4.63 us
    pallas_call x1, Pallas kernels, body(): call(project_kernel, jax.ShapeDtypeStruct((near * coded, HD), jnp.int16),...  2.65 us
    pallas_call x1, Pallas kernels, body(): call(functools.partial(attend_kernel, HD ** (-0.5), 1.0 / width_total), j...  2.13 us
  transfers between devices with their start and end apart: 1, of which 1 were waited for; matrix products, arithmetic and copies ran while one was open for 2% of the time, Pallas kernels for 0%

profile of v4, /device:TPU:1, one launch (start us, length us, event | category | flops | bytes accessed | tf_op | source)
XLA Modules:
  0.0 98.4 jit_solution(6984090703554311991)
XLA Ops:
  0.0 0.0 copy-start.5
  0.0 0.0 copy-start.4
  0.0 0.0 copy-start.3
  0.0 0.0 copy-start.2
  0.0 2.7 %project.1 = s16[1280,128]{1,0:T(8,128)(2,1)} custom-call(bf16[2,4,256]{2,1,0:T(4,128)(2,1)} %hidden_hbm.1, bf16[256]{0:T(256)(128)(2,1)} %gain_hbm.1, bf16[256,2048]{1,0:T(8,128)(2,1)} %wq_hbm.1, bf16[256,256]{1,0:T(8,128)(2,1)} %wkv_hbm.1), custom_call_target="tpu_custom_call" | custom-call | tf_op jit(solution)/shard_map/project/pallas_call | solution.py:330
  2.7 10.2 %all-to-all-start = ((s16[8,160,128]{2,1,0:T(8,128)(2,1)}), s16[8,160,128]{2,1,0:T(8,128)(2,1)S(1)}, u32[]{:S(2)}, u32[]{:S(2)}) async-start(s16[8,160,128]{2,1,0:T(8,128)(2,1)} %bitcast.24), calls=%async_computation | async-start | bytes 655360 | tf_op jit(solution)/shard_map/all_to_all | solution.py:322
  12.9 0.0 copy-done.3
  13.0 0.1 convert_element_type.14
  13.0 0.1 subtract_clamp_fusion
  13.1 0.0 copy-done.5
  13.1 0.0 copy-done.4
  13.2 0.0 copy-done.2
  13.2 0.3 select_reduce_fusion
  13.5 1.7 %fusion.1 = (bf16[4096,128]{1,0:T(8,128)(2,1)S(1)}, bf16[4096,128]{1,0:T(8,128)(2,1)S(1)}) fusion(bf16[4096,256]{1,0:T(8,128)(2,1)} %bitcast.23), kind=kLoop, calls=%fused_computation.15 | loop fusion | bytes 4194304 | tf_op jit(solution)/shard_map/slice | solution.py:365
  15.2 0.1 fusion
  15.3 0.1 pad_maximum_fusion
  15.4 4.6 %all-to-all-done = s16[8,160,128]{2,1,0:T(8,128)(2,1)S(1)} async-done(((s16[8,160,128]{2,1,0:T(8,128)(2,1)}), s16[8,160,128]{2,1,0:T(8,128)(2,1)S(1)}, u32[]{:S(2)}, u32[]{:S(2)}) %all-to-all-start) | async-done | bytes 327712 | tf_op jit(solution)/shard_map/all_to_all | solution.py:322
  20.0 0.3 sum.1
  20.3 16.5 %all_to_all.34 = s16[8,160,128]{2,1,0:T(8,128)(2,1)S(1)} all-to-all(s16[8,160,128]{2,1,0:T(8,128)(2,1)S(1)} %bitcast.14), channel_id=1, replica_groups=mesh['z'=8,'xc'=8,'head'=8] {'z'}, dimensions={0} | all-to-all | bytes 655360 | tf_op jit(solution)/shard_map/all_to_all | solution.py:322
  36.8 0.0 copy-start
  36.8 2.1 %attend.1 = bf16[1152,128]{1,0:T(8,128)(2,1)S(1)} custom-call(s16[1280,128]{1,0:T(8,128)(2,1)S(1)} %bitcast.15, f32[8,128]{1,0:T(8,128)S(1)} %get-tuple-element.20.cos_ref, f32[8,128]{1,0:T(8,128)S(1)} %get-tuple-element.21.sin_ref, s32[8,128]{1,0:T(8,128)S(1)} %pad_add_fusion.limit_ref, bf16[4096,128]{1,0:T(8,128)(2,1)S(1)} %get-tuple-element.23.keys_ref, ...), custom_call_target="tpu_custom_call" | custom-call | tf_op jit(solution)/shard_map/attend/pallas_call | solution.py:378
  38.9 0.0 copy-start.1
  38.9 12.9 %all_to_all.35 = bf16[8,144,128]{2,1,0:T(8,128)(2,1)S(1)} all-to-all(bf16[8,144,128]{2,1,0:T(8,128)(2,1)S(1)} %bitcast.18), channel_id=1, replica_groups=mesh['z'=8,'xc'=8,'head'=8] {'xc'}, dimensions={0} | all-to-all | bytes 589824 | tf_op jit(solution)/shard_map/all_to_all | solution.py:322
  51.8 0.3 merge.1
  52.1 14.7 %all_to_all.36 = bf16[8,144,128]{2,1,0:T(8,128)(2,1)S(1)} all-to-all(bf16[8,144,128]{2,1,0:T(8,128)(2,1)S(1)} %bitcast.17), channel_id=1, replica_groups=mesh['z'=8,'xc'=8,'head'=8] {'z'}, dimensions={0} | all-to-all | bytes 589824 | tf_op jit(solution)/shard_map/all_to_all | solution.py:322
  66.8 0.0 copy-done
  66.8 0.5 output.1
  67.3 13.8 %all_to_all.37 = f32[8,8,256]{2,1,0:T(8,128)S(1)} all-to-all(f32[8,8,256]{2,1,0:T(8,128)S(1)} %bitcast.20), channel_id=1, replica_groups=mesh['z'=8,'xc'=8,'head'=8] {'head'}, dimensions={0} | all-to-all | bytes 131072 | tf_op jit(solution)/shard_map/all_to_all | solution.py:322
  81.2 0.0 copy-done.1
  81.2 0.6 deliver.1
  81.7 16.0 %all_to_all.38 = bf16[2,64,256]{2,0,1:T(2,128)(2,1)S(1)} all-to-all(bf16[2,64,256]{2,0,1:T(2,128)(2,1)S(1)} %bitcast.22), channel_id=1, replica_groups=mesh['z'=8,'xc'=8,'head'=8] {'z','xc'}, dimensions={1} | all-to-all | bytes 131072 | tf_op jit(solution)/shard_map/all_to_all | solution.py:322
  97.7 0.6 copy.17
  (7 shorter events, 0.1 us)
Async XLA Ops:
  0.0 13.1 %copy-start.5 = (pred[128]{0:T(512)(128)(4,1)S(1)}, pred[128]{0:T(512)(128)(4,1)}, u32[]{:S(2)}) copy-start(pred[128]{0:T(512)(128)(4,1)} %constant.53.clone) | copy-start | bytes 388
  0.0 13.1 %copy-start.4 = (pred[128]{0:T(512)(128)(4,1)S(1)}, pred[128]{0:T(512)(128)(4,1)}, u32[]{:S(2)}) copy-start(pred[128]{0:T(512)(128)(4,1)} %constant.51.clone) | copy-start | bytes 388
  0.0 12.9 %copy-start.3 = (s32[4]{0:T(128)S(1)}, s32[4]{0:T(128)}, u32[]{:S(2)}) copy-start(s32[4]{0:T(128)} %param.20) | copy-start | bytes 52
  0.0 13.1 %copy-start.2 = (s32[4,256]{1,0:T(4,128)S(1)}, s32[4,256]{1,0:T(4,128)}, u32[]{:S(2)}) copy-start(s32[4,256]{1,0:T(4,128)} %param.19) | copy-start | bytes 12292
  2.7 17.4 %all-to-all-start = ((s16[8,160,128]{2,1,0:T(8,128)(2,1)}), s16[8,160,128]{2,1,0:T(8,128)(2,1)S(1)}, u32[]{:S(2)}, u32[]{:S(2)}) async-start(s16[8,160,128]{2,1,0:T(8,128)(2,1)} %bitcast.24), calls=%async_computation | async-start | bytes 655360 | tf_op jit(solution)/shard_map/all_to_all | solution.py:322
  36.8 30.1 %copy-start = (bf16[2048,256]{1,0:T(8,128)(2,1)S(1)}, bf16[2048,256]{1,0:T(8,128)(2,1)}, u32[]{:S(2)}) copy-start(bf16[2048,256]{1,0:T(8,128)(2,1)} %w_ref.1) | copy-start | bytes 3145732
  38.9 42.3 %copy-start.1 = (s32[4]{0:T(128)S(1)}, s32[4]{0:T(128)}, u32[]{:S(2)}) copy-start(s32[4]{0:T(128)} %owners_ref.1) | copy-start | bytes 52

commit v5 on v4

--- a/solution.py
+++ b/solution.py
@@ -150,26 +150,36 @@
     encode(heads, rest, out_ref)
 
 
-def sum_kernel(heads, parts_ref, out_ref):
-    encode(*decode(parts_ref, heads), out_ref)
-
-
-def attend_kernel(
-    scale, inverse_width, parts_ref, cos_ref, sin_ref, limit_ref, keys_ref, values_ref, out_ref,
-    score_ref,
-):
-    rows = HD
-    queries, (key, value, square) = decode(parts_ref, rows // 8)
+def half(core_ref, tiles):
+    n = len(tiles) // 2
+    return [jnp.where(core_ref[0] == 0, a, b) for a, b in zip(tiles[:n], tiles[n:])]
+
+
+def sum_kernel(heads, core_ref, parts_ref, out_ref):
+    queries, rest = decode(parts_ref, heads)
+    encode(half(core_ref, queries), rest, out_ref)
+
+
+def turn_kernel(scale, inverse_width, parts_ref, cos_ref, sin_ref, out_ref):
+    queries, (key, value, square) = decode(parts_ref, (out_ref.shape[0] - 16) // 8)
     root = lax.rsqrt(square * inverse_width + EPSILON)
 
     def turn(x):
         x = x * root
         return x * cos_ref[...] + pltpu.roll(x, HALF, 1) * sin_ref[...]
 
-    query = jnp.concatenate([turn(x) for x in queries], axis=0)
+    rows = [turn(x) * scale for x in queries] + [turn(key), value * root]
+    for k, x in enumerate(rows):
+        out_ref[8 * k : 8 * k + 8, :] = x
+
+
+def attend_kernel(rows_ref, limit_ref, keys_ref, values_ref, out_ref, score_ref):
+    rows = HD
+    span = rows_ref.shape[0] // 2
+    query = jnp.concatenate([rows_ref[0 : span - 16, :], rows_ref[span : 2 * span - 16, :]], axis=0)
     query = jnp.concatenate(split2(query), axis=0)
-    new_keys = turn(key)
-    new_values = value * root
+    new_keys = rows_ref[span - 16 : span - 8, :]
+    new_values = rows_ref[span - 8 : span, :]
     new_keys, new_values = [
         jnp.concatenate(pair, axis=0).astype(BF16)
         for pair in ((new_keys, new_values), (new_values, new_keys))
@@ -181,7 +191,7 @@
 
     def score(keys):
         both = dot_t(query, keys)
-        return (both[:rows] + both[rows:]) * scale
+        return both[:rows] + both[rows:]
 
     def mix(weights, values):
         both = dot(jnp.concatenate(split2(weights), axis=0), values)
@@ -246,8 +256,7 @@
         out_ref[k * block + rows : (k + 1) * block, :] = stats
 
 
-def merge(parts_ref):
-    rows = HD
+def merge(parts_ref, rows):
     block = rows + STATS
     peers = parts_ref.shape[0] // block
     tops, totals = [], []
@@ -271,24 +280,28 @@
     return mixed, top, total
 
 
-def merge_kernel(parts_ref, out_ref):
-    mixed, top, total = merge(parts_ref)
-    live = iota((8, HD), 1) < GROUP
-    post(
-        jnp.concatenate(mixed, axis=0), jnp.where(live, top, 0.0), jnp.where(live, total, 0.0), out_ref
-    )
-
-
-def output_kernel(parts_ref, w_ref, out_ref):
-    mixed, _, total = merge(parts_ref)
-    inverse = 1.0 / jnp.where(iota((8, HD), 1) < GROUP, total, 1.0)
-    lhs = jnp.concatenate(
-        [
-            mixed[h // 2][8 * (h % 2) : 8 * (h % 2) + 8] * inverse[:, h : h + 1]
-            for h in range(2 * len(mixed))
-        ],
-        axis=1,
-    )
+def merge_kernel(core_ref, parts_ref, out_ref):
+    mixed, top, total = merge(parts_ref, HD)
+    live = iota((8, HD), 1) < GROUP // 2
+    stats = []
+    for x in (top, total):
+        x = jnp.where(core_ref[0] == 0, x, pltpu.roll(x, HD - GROUP // 2, 1))
+        stats.append(jnp.where(live, x, 0.0))
+    post(jnp.concatenate(half(core_ref, mixed), axis=0), *stats, out_ref)
+
+
+def divide_kernel(parts_ref, out_ref):
+    heads = out_ref.shape[0] // 8
+    mixed, _, total = merge(parts_ref, 8 * heads)
+    inverse = 1.0 / jnp.where(iota((8, HD), 1) < heads, total, 1.0)
+    for h in range(heads):
+        row = mixed[h // 2][8 * (h % 2) : 8 * (h % 2) + 8]
+        out_ref[8 * h : 8 * h + 8, :] = row * inverse[:, h : h + 1]
+
+
+def output_kernel(rows_ref, w_ref, out_ref):
+    heads = rows_ref.shape[0] // 8
+    lhs = jnp.concatenate([rows_ref[8 * h : 8 * h + 8, :] for h in range(heads)], axis=1)
     part = dot(jnp.concatenate(split2(lhs), axis=0), w_ref[...])
     part = part[0:8] + part[8:16]
     for k in range(out_ref.shape[0] // 8):
@@ -309,8 +322,8 @@
 
 def body(hidden, norm_gain, w_query, w_keyval, w_out, cache, page_table, lengths, owners):
     n_steps, n_reqs, width_local = hidden.shape
-    ctx = ("z", "xc")
-    far, near = lax.axis_size("z"), lax.axis_size("xc")
+    ctx, around = ("z", "x", "core"), ("x", "core")
+    far, near = lax.axis_size("z"), lax.axis_size(around)
     peers = far * near
     groups = lax.axis_size("head")
     device_now = lax.axis_index(ctx)
@@ -323,7 +336,9 @@
 
     heads = w_query.shape[1] // HD
     coded = TILE * (heads // 2 + 2)
-    block = 8 * heads + STATS
+    coded_half = TILE * (heads // 4 + 2)
+    block, block_half = 8 * heads + STATS, 4 * heads + STATS
+    core = lax.axis_index("core").astype(jnp.int32).reshape(1)
 
     with jax.named_scope("project"):
         chunks = 4
@@ -343,7 +358,7 @@
     parts, lengths, page_table, cache = lax.optimization_barrier(
         (parts, lengths, page_table, cache)
     )
-    parts = exchange(parts.reshape(near, coded, HD), "xc").reshape(near * coded, HD)
+    parts = exchange(parts.reshape(near, coded, HD), around).reshape(near * coded, HD)
 
     position = (lengths[None, :] + jnp.arange(n_steps, dtype=jnp.int32)[:, None]).astype(F32)
     angles = position.reshape(n_steps * n_reqs, 1) * frequencies(HD)
@@ -370,29 +385,39 @@
     with jax.named_scope("sum"):
         parts = call(
             functools.partial(sum_kernel, heads),
-            jax.ShapeDtypeStruct((far * coded, HD), jnp.int16),
-            [vmem],
-        )(parts)
-    parts = exchange(parts.reshape(far, coded, HD), "z").reshape(far * coded, HD)
+            jax.ShapeDtypeStruct((far * coded_half, HD), jnp.int16),
+            [smem, vmem],
+        )(core, parts)
+    parts = exchange(parts.reshape(far, coded_half, HD), "z").reshape(far * coded_half, HD)
+    with jax.named_scope("turn"):
+        rows = call(
+            functools.partial(turn_kernel, HD ** (-0.5), 1.0 / width_total),
+            jax.ShapeDtypeStruct((4 * heads + 16, HD), F32),
+            [vmem] * 3,
+        )(parts, cosine, sine)
+    rows = lax.all_gather(rows, "core", axis=0, tiled=True)
     with jax.named_scope("attend"):
         parts = call(
-            functools.partial(attend_kernel, HD ** (-0.5), 1.0 / width_total),
+            attend_kernel,
             jax.ShapeDtypeStruct((near * block, HD), BF16),
-            [vmem] * 6,
+            [vmem] * 4,
             scratch=[pltpu.VMEM((8 * heads, pages * page_len), F32)],
-        )(parts, cosine, sine, limit, keys, values)
-    parts = exchange(parts.reshape(near, block, HD), "xc").reshape(near * block, HD)
+        )(rows, limit, keys, values)
+    parts = exchange(parts.reshape(near, block, HD), around).reshape(near * block, HD)
     with jax.named_scope("merge"):
         parts = call(
-            merge_kernel, jax.ShapeDtypeStruct((far * block, HD), BF16), [vmem]
-        )(parts)
-    parts = exchange(parts.reshape(far, block, HD), "z").reshape(far * block, HD)
+            merge_kernel, jax.ShapeDtypeStruct((far * block_half, HD), BF16), [smem, vmem]
+        )(core, parts)
+    parts = exchange(parts.reshape(far, block_half, HD), "z").reshape(far * block_half, HD)
+    with jax.named_scope("divide"):
+        rows = call(divide_kernel, jax.ShapeDtypeStruct((4 * heads, HD), F32), [vmem])(parts)
+    rows = lax.all_gather(rows, "core", axis=0, tiled=True)
     with jax.named_scope("output"):
         parts = call(
             output_kernel,
             jax.ShapeDtypeStruct((8 * groups, width_local), F32),
             [vmem] * 2,
-        )(parts, w_out)
+        )(rows, w_out)
     parts = exchange(parts.reshape(groups, 8, width_local), "head")
     with jax.named_scope("deliver"):
         sent = call(
@@ -402,11 +427,11 @@
 
 
 def solution(mesh):
-    ctx = ("z", "xc")
-    near = 8
+    ctx = ("z", "x", "core")
+    x, core = 4, 2
     split = Mesh(
-        mesh.devices.reshape(mesh.shape["ctx"] // near, near, mesh.shape["head"]),
-        ("z", "xc", "head"),
+        mesh.devices.reshape(mesh.shape["ctx"] // (x * core), x, core, mesh.shape["head"]),
+        ("z", "x", "core", "head"),
     )
     placed = (
         P(None, None, ctx),

time: 98.8 us -> 96.9 us (0.981)
  blocking collectives: 73.9 us -> 72 us
    all_to_all x5, blocking collectives: 73.9 us -> 64 us  [exchange(): return lax.all_to_all(x, axis, dim, dim, tiled=True)]
    all_gather x0 -> x2, blocking collectives: none -> 7.97 us  [body(): rows = lax.all_gather(rows, 'core', axis=0, tiled=True)]
    pallas_call x2 -> x4, Pallas kernels: 2.45 us -> 2.67 us  [the longest x1 1.88 us: body(): call(attend_kernel, jax.ShapeDtypeStruct((near * block, HD), BF16), [vmem...]
  transfers between devices with their start and end apart: 1 -> 1, of which waited for: 1 -> 1; matrix products, arithmetic and copies ran while one was open for 2% -> 3% of each run, Pallas kernels for 0% -> 0%
where the time goes in v5:
time: 96.9 us; the launch traced here: 96.4 us
  blocking collectives  72 us (74%)
  starting transfers between devices  10.2 us (11%)
  Pallas kernels  6.37 us (7%)
  waiting for transfers between devices  4.63 us (5%)
  local copies, waits for them, and re-layouts  2.42 us (2%)
    all_to_all x5, blocking collectives, exchange(): return lax.all_to_all(x, axis, dim, dim, tiled=True)  64 us
    all_to_all x1, starting transfers between devices, exchange(): return lax.all_to_all(x, axis, dim, dim, tiled=True)  10.2 us
    all_gather x2, blocking collectives, body(): rows = lax.all_gather(rows, 'core', axis=0, tiled=True)  7.97 us
    all_to_all x1, waiting for transfers between devices, exchange(): return lax.all_to_all(x, axis, dim, dim, tiled=True)  4.63 us
    pallas_call x1, Pallas kernels, body(): call(project_kernel, jax.ShapeDtypeStruct((near * coded, HD), jnp.int16),...  2.65 us
  transfers between devices with their start and end apart: 1, of which 1 were waited for; matrix products, arithmetic and copies ran while one was open for 3% of the time, Pallas kernels for 0%

profile of v5, /device:TPU:1, one launch (start us, length us, event | category | flops | bytes accessed | tf_op | source)
XLA Modules:
  0.0 96.4 jit_solution(1597227236464555234)
XLA Ops:
  0.0 0.0 copy-start.5
  0.0 0.0 copy-start.4
  0.0 0.0 copy-start.3
  0.0 0.0 copy-start.2
  0.0 2.7 %project.1 = s16[1280,128]{1,0:T(8,128)(2,1)} custom-call(bf16[2,4,256]{2,1,0:T(4,128)(2,1)} %hidden_hbm.1, bf16[256]{0:T(256)(128)(2,1)} %gain_hbm.1, bf16[256,2048]{1,0:T(8,128)(2,1)} %wq_hbm.1, bf16[256,256]{1,0:T(8,128)(2,1)} %wkv_hbm.1), custom_call_target="tpu_custom_call" | custom-call | tf_op jit(solution)/shard_map/project/pallas_call | solution.py:345
  2.7 10.2 %all-to-all-start = ((s16[8,160,128]{2,1,0:T(8,128)(2,1)}), s16[8,160,128]{2,1,0:T(8,128)(2,1)S(1)}, u32[]{:S(2)}, u32[]{:S(2)}) async-start(s16[8,160,128]{2,1,0:T(8,128)(2,1)} %bitcast.25), calls=%async_computation | async-start | bytes 655360 | tf_op jit(solution)/shard_map/all_to_all | solution.py:335
  12.9 0.0 copy-done.3
  13.0 0.1 convert_element_type.14
  13.1 0.1 subtract_clamp_fusion
  13.1 0.0 copy-done.5
  13.1 0.0 copy-done.4
  13.2 0.0 copy-done.2
  13.2 0.3 select_reduce_fusion
  13.5 1.7 %fusion.1 = (bf16[4096,128]{1,0:T(8,128)(2,1)S(1)}, bf16[4096,128]{1,0:T(8,128)(2,1)S(1)}) fusion(bf16[4096,256]{1,0:T(8,128)(2,1)} %bitcast.24), kind=kLoop, calls=%fused_computation.15 | loop fusion | bytes 4194304 | tf_op jit(solution)/shard_map/slice | solution.py:380
  15.2 0.1 fusion
  15.3 0.1 pad_maximum_fusion
  15.4 4.6 %all-to-all-done = s16[8,160,128]{2,1,0:T(8,128)(2,1)S(1)} async-done(((s16[8,160,128]{2,1,0:T(8,128)(2,1)}), s16[8,160,128]{2,1,0:T(8,128)(2,1)S(1)}, u32[]{:S(2)}, u32[]{:S(2)}) %all-to-all-start) | async-done | bytes 327712 | tf_op jit(solution)/shard_map/all_to_all | solution.py:335
  20.0 0.2 sum.1
  20.3 13.8 %all_to_all.34 = s16[8,96,128]{2,1,0:T(8,128)(2,1)S(1)} all-to-all(s16[8,96,128]{2,1,0:T(8,128)(2,1)S(1)} %bitcast.17), channel_id=1, replica_groups=mesh['z'=8,'x'=4,'core'=2,'head'=8] {'z'}, dimensions={0} | all-to-all | bytes 393216 | tf_op jit(solution)/shard_map/all_to_all | solution.py:335
  34.1 0.2 turn.1
  34.3 4.6 %all_gather.6.rows_ref = f32[160,128]{1,0:T(8,128)S(1)} all-gather(f32[80,128]{1,0:T(8,128)S(1)} %turn.1), channel_id=1, replica_groups=mesh['z'=8,'x'=4,'core'=2,'head'=8] {'core'}, dimensions={0}, use_global_device_ids=true | all-gather | bytes 122880 | tf_op jit(solution)/shard_map/all_gather | solution.py:398
  38.8 0.0 copy-start
  38.8 1.9 %attend.1 = bf16[1152,128]{1,0:T(8,128)(2,1)S(1)} custom-call(f32[160,128]{1,0:T(8,128)S(1)} %all_gather.6.rows_ref, s32[8,128]{1,0:T(8,128)S(1)} %pad_add_fusion.limit_ref, bf16[4096,128]{1,0:T(8,128)(2,1)S(1)} %get-tuple-element.23.keys_ref, bf16[4096,128]{1,0:T(8,128)(2,1)S(1)} %get-tuple-element.24.values_ref), custom_call_target="tpu_custom_call" | custom-call | tf_op jit(solution)/shard_map/attend/pallas_call | solution.py:400
  40.7 0.0 copy-start.1
  40.7 10.0 %all_to_all.35 = bf16[8,144,128]{2,1,0:T(8,128)(2,1)S(1)} all-to-all(bf16[8,144,128]{2,1,0:T(8,128)(2,1)S(1)} %bitcast.15), channel_id=1, replica_groups=mesh['z'=8,'x'=4,'core'=2,'head'=8] {'x','core'}, dimensions={0} | all-to-all | bytes 589824 | tf_op jit(solution)/shard_map/all_to_all | solution.py:335
  50.8 0.3 merge.1
  51.1 11.2 %all_to_all.36 = bf16[8,80,128]{2,1,0:T(8,128)(2,1)S(1)} all-to-all(bf16[8,80,128]{2,1,0:T(8,128)(2,1)S(1)} %bitcast.19), channel_id=1, replica_groups=mesh['z'=8,'x'=4,'core'=2,'head'=8] {'z'}, dimensions={0} | all-to-all | bytes 327680 | tf_op jit(solution)/shard_map/all_to_all | solution.py:335
  62.3 0.3 divide.1
  62.6 3.4 %all_gather.7.rows_ref = f32[128,128]{1,0:T(8,128)S(1)} all-gather(f32[64,128]{1,0:T(8,128)S(1)} %divide.1), channel_id=1, replica_groups=mesh['z'=8,'x'=4,'core'=2,'head'=8] {'core'}, dimensions={0}, use_global_device_ids=true | all-gather | bytes 98304 | tf_op jit(solution)/shard_map/all_gather | solution.py:414
  66.0 0.0 copy-done
  66.0 0.2 output.1
  66.2 13.9 %all_to_all.37 = f32[8,8,256]{2,1,0:T(8,128)S(1)} all-to-all(f32[8,8,256]{2,1,0:T(8,128)S(1)} %bitcast.21), channel_id=1, replica_groups=mesh['z'=8,'x'=4,'core'=2,'head'=8] {'head'}, dimensions={0} | all-to-all | bytes 131072 | tf_op jit(solution)/shard_map/all_to_all | solution.py:335
  80.1 0.0 copy-done.1
  80.1 0.6 deliver.1
  80.7 15.1 %all_to_all.38 = bf16[2,64,256]{2,0,1:T(2,128)(2,1)S(1)} all-to-all(bf16[2,64,256]{2,0,1:T(2,128)(2,1)S(1)} %bitcast.23), channel_id=1, replica_groups=mesh['z'=8,'x'=4,'core'=2,'head'=8] {'z','x','core'}, dimensions={1} | all-to-all | bytes 131072 | tf_op jit(solution)/shard_map/all_to_all | solution.py:335
  95.8 0.6 copy.17
  (7 shorter events, 0.1 us)
Async XLA Ops:
  0.0 13.1 %copy-start.5 = (pred[128]{0:T(512)(128)(4,1)S(1)}, pred[128]{0:T(512)(128)(4,1)}, u32[]{:S(2)}) copy-start(pred[128]{0:T(512)(128)(4,1)} %constant.62.clone) | copy-start | bytes 388
  0.0 13.1 %copy-start.4 = (pred[128]{0:T(512)(128)(4,1)S(1)}, pred[128]{0:T(512)(128)(4,1)}, u32[]{:S(2)}) copy-start(pred[128]{0:T(512)(128)(4,1)} %constant.60.clone) | copy-start | bytes 388
  0.0 12.9 %copy-start.3 = (s32[4]{0:T(128)S(1)}, s32[4]{0:T(128)}, u32[]{:S(2)}) copy-start(s32[4]{0:T(128)} %param.20) | copy-start | bytes 52
  0.0 13.2 %copy-start.2 = (s32[4,256]{1,0:T(4,128)S(1)}, s32[4,256]{1,0:T(4,128)}, u32[]{:S(2)}) copy-start(s32[4,256]{1,0:T(4,128)} %param.19) | copy-start | bytes 12292
  2.7 17.4 %all-to-all-start = ((s16[8,160,128]{2,1,0:T(8,128)(2,1)}), s16[8,160,128]{2,1,0:T(8,128)(2,1)S(1)}, u32[]{:S(2)}, u32[]{:S(2)}) async-start(s16[8,160,128]{2,1,0:T(8,128)(2,1)} %bitcast.25), calls=%async_computation | async-start | bytes 655360 | tf_op jit(solution)/shard_map/all_to_all | solution.py:335
  38.8 27.2 %copy-start = (bf16[2048,256]{1,0:T(8,128)(2,1)S(1)}, bf16[2048,256]{1,0:T(8,128)(2,1)}, u32[]{:S(2)}) copy-start(bf16[2048,256]{1,0:T(8,128)(2,1)} %w_ref.1) | copy-start | bytes 3145732
  40.7 39.4 %copy-start.1 = (s32[4]{0:T(128)S(1)}, s32[4]{0:T(128)}, u32[]{:S(2)}) copy-start(s32[4]{0:T(128)} %owners_ref.1) | copy-start | bytes 52

commit v6 on v4

--- a/solution.py
+++ b/solution.py
@@ -93,11 +93,11 @@
             out_ref[start : start + TILE, :] = pair
 
 
-def decode(parts_ref, heads):
+def decode(parts_ref, heads, first=0, step=1):
     pairs = heads // 2 + 2
     block = TILE * pairs
     sums = None
-    for n in range(parts_ref.shape[0] // block):
+    for n in range(first, parts_ref.shape[0] // block, step):
         tiles = [
             parts_ref[n * block + k * TILE : n * block + (k + 1) * TILE, :]
             .astype(jnp.int32)
@@ -147,7 +147,19 @@
         part = dot(lhs, wq_ref[:, k * chunk : (k + 1) * chunk])
         part = part[0:8] + part[8:16]
         heads += [part[:, g * HD : (g + 1) * HD] for g in range(chunk // HD)]
-    encode(heads, rest, out_ref)
+    for k, x in enumerate(heads + rest):
+        out_ref[8 * k : 8 * k + 8, :] = x
+
+
+def half(core_ref, tiles):
+    n = len(tiles) // 2
+    return [jnp.where(core_ref[0] == 0, a, b) for a, b in zip(tiles[:n], tiles[n:])]
+
+
+def pair_kernel(core_ref, rows_ref, out_ref):
+    n = rows_ref.shape[0] // 2
+    tiles = [rows_ref[k : k + 8, :] + rows_ref[n + k : n + k + 8, :] for k in range(0, n, 8)]
+    encode(half(core_ref, tiles[:-3]), tiles[-3:], out_ref)
 
 
 def sum_kernel(heads, parts_ref, out_ref):
@@ -159,17 +171,17 @@
     score_ref,
 ):
     rows = HD
-    queries, (key, value, square) = decode(parts_ref, rows // 8)
+    queries, (key, value, square) = decode(parts_ref, rows // 16, 0, 2)
+    queries += decode(parts_ref, rows // 16, 1, 2)[0]
     root = lax.rsqrt(square * inverse_width + EPSILON)
 
     def turn(x):
         x = x * root
         return x * cos_ref[...] + pltpu.roll(x, HALF, 1) * sin_ref[...]
 
-    query = jnp.concatenate([turn(x) for x in queries], axis=0)
+    query = jnp.concatenate([turn(x) * scale for x in queries], axis=0)
     query = jnp.concatenate(split2(query), axis=0)
-    new_keys = turn(key)
-    new_values = value * root
+    new_keys, new_values = turn(key), value * root
     new_keys, new_values = [
         jnp.concatenate(pair, axis=0).astype(BF16)
         for pair in ((new_keys, new_values), (new_values, new_keys))
@@ -181,7 +193,7 @@
 
     def score(keys):
         both = dot_t(query, keys)
-        return (both[:rows] + both[rows:]) * scale
+        return both[:rows] + both[rows:]
 
     def mix(weights, values):
         both = dot(jnp.concatenate(split2(weights), axis=0), values)
@@ -218,7 +230,8 @@
             sums = sums + weights[:, k * page : (k + 1) * page]
         mixed = mixed + mix(weights, values_ref[start : start + chunk, :])
     total = total + jnp.sum(sums, axis=-1, keepdims=True)
-    post(mixed, tiled(top), tiled(total), out_ref)
+    out_ref[0:rows, :] = mixed
+    out_ref[rows : rows + 8, :] = tiled(top) + pltpu.roll(tiled(total), GROUP, 1)
 
 
 STATS = 16
@@ -246,12 +259,11 @@
         out_ref[k * block + rows : (k + 1) * block, :] = stats
 
 
-def merge(parts_ref):
-    rows = HD
+def merge(parts_ref, rows, first=0, step=1):
     block = rows + STATS
-    peers = parts_ref.shape[0] // block
+    peers = range(first, parts_ref.shape[0] // block, step)
     tops, totals = [], []
-    for k in range(peers):
+    for k in peers:
         tile = parts_ref[k * block + rows : (k + 1) * block, :].astype(F32)[0:8]
         tile = tile + pltpu.roll(tile, HD - GROUP, 1) + pltpu.roll(tile, HD - 2 * GROUP, 1)
         tops.append(tile)
@@ -262,33 +274,52 @@
     mixed = []
     for g in range(rows // 16):
         acc = None
-        for k in range(peers):
+        for k, f in zip(peers, factors):
             part = parts_ref[k * block + 16 * g : k * block + 16 * g + 16, :].astype(F32)
-            f = factors[k]
             f = jnp.concatenate([f[:, 2 * g : 2 * g + 1], f[:, 2 * g + 1 : 2 * g + 2]], axis=0)
             acc = f * part if acc is None else acc + f * part
         mixed.append(acc)
     return mixed, top, total
 
 
-def merge_kernel(parts_ref, out_ref):
-    mixed, top, total = merge(parts_ref)
-    live = iota((8, HD), 1) < GROUP
-    post(
-        jnp.concatenate(mixed, axis=0), jnp.where(live, top, 0.0), jnp.where(live, total, 0.0), out_ref
-    )
-
-
-def output_kernel(parts_ref, w_ref, out_ref):
-    mixed, _, total = merge(parts_ref)
-    inverse = 1.0 / jnp.where(iota((8, HD), 1) < GROUP, total, 1.0)
-    lhs = jnp.concatenate(
-        [
-            mixed[h // 2][8 * (h % 2) : 8 * (h % 2) + 8] * inverse[:, h : h + 1]
-            for h in range(2 * len(mixed))
-        ],
-        axis=1,
-    )
+def join_kernel(core_ref, rows_ref, out_ref):
+    n = rows_ref.shape[0] // 2
+    tops = [rows_ref[k * n + n - 8 : k * n + n, :] for k in range(2)]
+    totals = [pltpu.roll(x, HD - GROUP, 1) for x in tops]
+    top = jnp.maximum(tops[0], tops[1])
+    factors = [jnp.exp(x - top) for x in tops]
+    total = factors[0] * totals[0] + factors[1] * totals[1]
+    mixed = [
+        sum(
+            factors[k][:, h : h + 1] * rows_ref[k * n + 8 * h : k * n + 8 * h + 8, :]
+            for k in range(2)
+        )
+        for h in range(n // 8 - 1)
+    ]
+    live = iota((8, HD), 1) < GROUP // 2
+    stats = []
+    for x in (top, total):
+        x = jnp.where(core_ref[0] == 0, x, pltpu.roll(x, HD - GROUP // 2, 1))
+        stats.append(jnp.where(live, x, 0.0))
+    post(jnp.concatenate(half(core_ref, mixed), axis=0), *stats, out_ref)
+
+
+def merge_kernel(heads, parts_ref, out_ref):
+    mixed, top, total = merge(parts_ref, 8 * heads)
+    live = iota((8, HD), 1) < heads
+    stats = [jnp.where(live, x, 0.0) for x in (top, total)]
+    post(jnp.concatenate(mixed, axis=0), *stats, out_ref)
+
+
+def output_kernel(heads, parts_ref, w_ref, out_ref):
+    lhs = []
+    for core in range(2):
+        mixed, _, total = merge(parts_ref, 8 * heads, core, 2)
+        inverse = 1.0 / jnp.where(iota((8, HD), 1) < heads, total, 1.0)
+        for h in range(heads):
+            row = mixed[h // 2][8 * (h % 2) : 8 * (h % 2) + 8]
+            lhs.append(row * inverse[:, h : h + 1])
+    lhs = jnp.concatenate(lhs, axis=1)
     part = dot(jnp.concatenate(split2(lhs), axis=0), w_ref[...])
     part = part[0:8] + part[8:16]
     for k in range(out_ref.shape[0] // 8):
@@ -309,8 +340,8 @@
 
 def body(hidden, norm_gain, w_query, w_keyval, w_out, cache, page_table, lengths, owners):
     n_steps, n_reqs, width_local = hidden.shape
-    ctx = ("z", "xc")
-    far, near = lax.axis_size("z"), lax.axis_size("xc")
+    ctx, around = ("z", "x", "core"), ("x", "core")
+    far, near = lax.axis_size("z"), lax.axis_size(around)
     peers = far * near
     groups = lax.axis_size("head")
     device_now = lax.axis_index(ctx)
@@ -322,14 +353,14 @@
         return lax.all_to_all(x, axis, dim, dim, tiled=True)
 
     heads = w_query.shape[1] // HD
-    coded = TILE * (heads // 2 + 2)
-    block = 8 * heads + STATS
+    coded, block = TILE * (heads // 4 + 2), 4 * heads + STATS
+    core = lax.axis_index("core").astype(jnp.int32).reshape(1)
 
     with jax.named_scope("project"):
         chunks = 4
         parts = call(
             project_kernel,
-            jax.ShapeDtypeStruct((near * coded, HD), jnp.int16),
+            jax.ShapeDtypeStruct((8 * (heads + 3), HD), F32),
             [hbm] * 4,
             scratch=[
                 pltpu.VMEM(hidden.shape, BF16),
@@ -340,10 +371,15 @@
             ],
             limit=60,
         )(hidden, norm_gain, w_query, w_keyval)
+    parts = lax.all_gather(parts, "core", axis=0, tiled=True)
+    with jax.named_scope("pair"):
+        parts = call(
+            pair_kernel, jax.ShapeDtypeStruct((far * coded, HD), jnp.int16), [smem, vmem]
+        )(core, parts)
     parts, lengths, page_table, cache = lax.optimization_barrier(
         (parts, lengths, page_table, cache)
     )
-    parts = exchange(parts.reshape(near, coded, HD), "xc").reshape(near * coded, HD)
+    parts = exchange(parts.reshape(far, coded, HD), "z").reshape(far * coded, HD)
 
     position = (lengths[None, :] + jnp.arange(n_steps, dtype=jnp.int32)[:, None]).astype(F32)
     angles = position.reshape(n_steps * n_reqs, 1) * frequencies(HD)
@@ -369,27 +405,34 @@
 
     with jax.named_scope("sum"):
         parts = call(
-            functools.partial(sum_kernel, heads),
-            jax.ShapeDtypeStruct((far * coded, HD), jnp.int16),
+            functools.partial(sum_kernel, heads // 2),
+            jax.ShapeDtypeStruct((near * coded, HD), jnp.int16),
             [vmem],
         )(parts)
-    parts = exchange(parts.reshape(far, coded, HD), "z").reshape(far * coded, HD)
+    parts = exchange(parts.reshape(near, coded, HD), around).reshape(near * coded, HD)
     with jax.named_scope("attend"):
         parts = call(
             functools.partial(attend_kernel, HD ** (-0.5), 1.0 / width_total),
-            jax.ShapeDtypeStruct((near * block, HD), BF16),
+            jax.ShapeDtypeStruct((8 * heads + 8, HD), F32),
             [vmem] * 6,
             scratch=[pltpu.VMEM((8 * heads, pages * page_len), F32)],
         )(parts, cosine, sine, limit, keys, values)
-    parts = exchange(parts.reshape(near, block, HD), "xc").reshape(near * block, HD)
+    parts = lax.all_gather(parts, "core", axis=0, tiled=True)
+    with jax.named_scope("join"):
+        parts = call(
+            join_kernel, jax.ShapeDtypeStruct((far * block, HD), BF16), [smem, vmem]
+        )(core, parts)
+    parts = exchange(parts.reshape(far, block, HD), "z").reshape(far * block, HD)
     with jax.named_scope("merge"):
         parts = call(
-            merge_kernel, jax.ShapeDtypeStruct((far * block, HD), BF16), [vmem]
+            functools.partial(merge_kernel, heads // 2),
+            jax.ShapeDtypeStruct((near * block, HD), BF16),
+            [vmem],
         )(parts)
-    parts = exchange(parts.reshape(far, block, HD), "z").reshape(far * block, HD)
+    parts = exchange(parts.reshape(near, block, HD), around).reshape(near * block, HD)
     with jax.named_scope("output"):
         parts = call(
-            output_kernel,
+            functools.partial(output_kernel, heads // 2),
             jax.ShapeDtypeStruct((8 * groups, width_local), F32),
             [vmem] * 2,
         )(parts, w_out)
@@ -402,11 +445,11 @@
 
 
 def solution(mesh):
-    ctx = ("z", "xc")
-    near = 8
+    ctx = ("z", "x", "core")
+    x, core = 4, 2
     split = Mesh(
-        mesh.devices.reshape(mesh.shape["ctx"] // near, near, mesh.shape["head"]),
-        ("z", "xc", "head"),
+        mesh.devices.reshape(mesh.shape["ctx"] // (x * core), x, core, mesh.shape["head"]),
+        ("z", "x", "core", "head"),
     )
     placed = (
         P(None, None, ctx),

time: 98.8 us -> 96.1 us (0.973)
  starting transfers between devices: 10.2 us -> 4.66 us
  waiting for transfers between devices: 4.63 us -> 6.94 us
    all_gather x0 -> x2, blocking collectives: none -> 11.2 us  [body(): parts = lax.all_gather(parts, 'core', axis=0, tiled=True)]
    all_to_all x5, blocking collectives: 73.9 us -> 62.7 us  [exchange(): return lax.all_to_all(x, axis, dim, dim, tiled=True)]
    all_to_all x1, starting transfers between devices: 10.2 us -> 4.66 us  [exchange(): return lax.all_to_all(x, axis, dim, dim, tiled=True)]
    all_to_all x1, waiting for transfers between devices: 4.63 us -> 6.94 us  [exchange(): return lax.all_to_all(x, axis, dim, dim, tiled=True)]
    pallas_call x4 -> x6, Pallas kernels: 3.74 us -> 4.4 us  [the longest x1 2.42 us: body(): call(project_kernel, jax.ShapeDtypeStruct((8 * (heads + 3), HD), F32), [h...]
  transfers between devices with their start and end apart: 1 -> 1, of which waited for: 1 -> 1; matrix products, arithmetic and copies ran while one was open for 2% -> 3% of each run, Pallas kernels for 0% -> 0%
where the time goes in v6:
time: 96.1 us; the launch traced here: 95.7 us
  blocking collectives  73.9 us (77%)
  Pallas kernels  6.99 us (7%)
  waiting for transfers between devices  6.94 us (7%)
  starting transfers between devices  4.66 us (5%)
  local copies, waits for them, and re-layouts  2.42 us (3%)
    all_to_all x5, blocking collectives, exchange(): return lax.all_to_all(x, axis, dim, dim, tiled=True)  62.7 us
    all_gather x2, blocking collectives, body(): parts = lax.all_gather(parts, 'core', axis=0, tiled=True)  11.2 us
    all_to_all x1, waiting for transfers between devices, exchange(): return lax.all_to_all(x, axis, dim, dim, tiled=True)  6.94 us
    all_to_all x1, starting transfers between devices, exchange(): return lax.all_to_all(x, axis, dim, dim, tiled=True)  4.66 us
    pallas_call x1, Pallas kernels, body(): call(project_kernel, jax.ShapeDtypeStruct((8 * (heads + 3), HD), F32), [h...  2.42 us
    pallas_call x1, Pallas kernels, body(): call(functools.partial(attend_kernel, HD ** (-0.5), 1.0 / width_total), j...  2.03 us
  transfers between devices with their start and end apart: 1, of which 1 were waited for; matrix products, arithmetic and copies ran while one was open for 3% of the time, Pallas kernels for 0%

profile of v6, /device:TPU:1, one launch (start us, length us, event | category | flops | bytes accessed | tf_op | source)
XLA Modules:
  0.0 95.7 jit_solution(5251773351657801861)
XLA Ops:
  0.0 0.0 copy-start.5
  0.0 0.0 copy-start.4
  0.0 0.0 copy-start.3
  0.0 0.0 copy-start.2
  0.0 2.4 %project.1 = f32[152,128]{1,0:T(8,128)} custom-call(bf16[2,4,256]{2,1,0:T(4,128)(2,1)} %hidden_hbm.1, bf16[256]{0:T(256)(128)(2,1)} %gain_hbm.1, bf16[256,2048]{1,0:T(8,128)(2,1)} %wq_hbm.1, bf16[256,256]{1,0:T(8,128)(2,1)} %wkv_hbm.1), custom_call_target="tpu_custom_call" | custom-call | tf_op jit(solution)/shard_map/project/pallas_call | solution.py:361
  2.5 8.7 %all_gather.6.rows_ref = f32[304,128]{1,0:T(8,128)S(1)} all-gather(f32[152,128]{1,0:T(8,128)} %project.1), channel_id=1, replica_groups=mesh['z'=8,'x'=4,'core'=2,'head'=8] {'core'}, dimensions={0}, use_global_device_ids=true | all-gather | bytes 233472 | tf_op jit(solution)/shard_map/all_gather | solution.py:374
  11.1 0.8 pair.1
  11.9 4.7 %all-to-all-start = ((s16[8,96,128]{2,1,0:T(8,128)(2,1)}), s16[8,96,128]{2,1,0:T(8,128)(2,1)S(1)}, u32[]{:S(2)}, u32[]{:S(2)}) async-start(s16[8,96,128]{2,1,0:T(8,128)(2,1)} %bitcast.1), calls=%async_computation | async-start | bytes 393216 | tf_op jit(solution)/shard_map/all_to_all | solution.py:353
  16.6 0.0 copy-done.3
  16.6 0.1 subtract_clamp_fusion
  16.7 0.0 copy-done.5
  16.7 0.0 copy-done.4
  16.7 0.0 copy-done.2
  16.7 0.3 select_reduce_fusion
  17.1 1.7 %fusion.1 = (bf16[4096,128]{1,0:T(8,128)(2,1)S(1)}, bf16[4096,128]{1,0:T(8,128)(2,1)S(1)}) fusion(bf16[4096,256]{1,0:T(8,128)(2,1)} %bitcast.24), kind=kLoop, calls=%fused_computation.15 | loop fusion | bytes 4194304 | tf_op jit(solution)/shard_map/slice | solution.py:401
  18.8 0.1 convert_element_type.14
  18.9 0.1 fusion
  19.0 0.1 pad_maximum_fusion
  19.1 6.9 %all-to-all-done = s16[8,96,128]{2,1,0:T(8,128)(2,1)S(1)} async-done(((s16[8,96,128]{2,1,0:T(8,128)(2,1)}), s16[8,96,128]{2,1,0:T(8,128)(2,1)S(1)}, u32[]{:S(2)}, u32[]{:S(2)}) %all-to-all-start) | async-done | bytes 196640 | tf_op jit(solution)/shard_map/all_to_all | solution.py:353
  26.0 0.2 sum.1
  26.3 0.0 copy-start
  26.3 12.1 %all_to_all.34 = s16[8,96,128]{2,1,0:T(8,128)(2,1)S(1)} all-to-all(s16[8,96,128]{2,1,0:T(8,128)(2,1)S(1)} %bitcast.16), channel_id=1, replica_groups=mesh['z'=8,'x'=4,'core'=2,'head'=8] {'x','core'}, dimensions={0} | all-to-all | bytes 393216 | tf_op jit(solution)/shard_map/all_to_all | solution.py:353
  38.4 0.0 copy-start.1
  38.4 2.0 %attend.1 = f32[136,128]{1,0:T(8,128)S(1)} custom-call(s16[768,128]{1,0:T(8,128)(2,1)S(1)} %bitcast.14, f32[8,128]{1,0:T(8,128)S(1)} %get-tuple-element.20.cos_ref, f32[8,128]{1,0:T(8,128)S(1)} %get-tuple-element.21.sin_ref, s32[8,128]{1,0:T(8,128)S(1)} %pad_add_fusion.limit_ref, bf16[4096,128]{1,0:T(8,128)(2,1)S(1)} %get-tuple-element.23.keys_ref, ...), custom_call_target="tpu_custom_call" | custom-call | tf_op jit(solution)/shard_map/attend/pallas_call | solution.py:414
  40.4 2.5 %all_gather.7.rows_ref = f32[272,128]{1,0:T(8,128)S(1)} all-gather(f32[136,128]{1,0:T(8,128)S(1)} %attend.1), channel_id=1, replica_groups=mesh['z'=8,'x'=4,'core'=2,'head'=8] {'core'}, dimensions={0}, use_global_device_ids=true | all-gather | bytes 208896 | tf_op jit(solution)/shard_map/all_gather | solution.py:420
  42.9 0.2 join.1
  43.1 11.6 %all_to_all.35 = bf16[8,80,128]{2,1,0:T(8,128)(2,1)S(1)} all-to-all(bf16[8,80,128]{2,1,0:T(8,128)(2,1)S(1)} %bitcast.18), channel_id=1, replica_groups=mesh['z'=8,'x'=4,'core'=2,'head'=8] {'z'}, dimensions={0} | all-to-all | bytes 327680 | tf_op jit(solution)/shard_map/all_to_all | solution.py:353
  54.7 0.3 merge.1
  55.0 9.5 %all_to_all.36 = bf16[8,80,128]{2,1,0:T(8,128)(2,1)S(1)} all-to-all(bf16[8,80,128]{2,1,0:T(8,128)(2,1)S(1)} %bitcast.20), channel_id=1, replica_groups=mesh['z'=8,'x'=4,'core'=2,'head'=8] {'x','core'}, dimensions={0} | all-to-all | bytes 327680 | tf_op jit(solution)/shard_map/all_to_all | solution.py:353
  64.5 0.0 copy-done
  64.5 0.5 output.1
  65.0 13.9 %all_to_all.37 = f32[8,8,256]{2,1,0:T(8,128)S(1)} all-to-all(f32[8,8,256]{2,1,0:T(8,128)S(1)} %bitcast.21), channel_id=1, replica_groups=mesh['z'=8,'x'=4,'core'=2,'head'=8] {'head'}, dimensions={0} | all-to-all | bytes 131072 | tf_op jit(solution)/shard_map/all_to_all | solution.py:353
  78.8 0.0 copy-done.1
  78.8 0.6 deliver.1
  79.4 15.7 %all_to_all.38 = bf16[2,64,256]{2,0,1:T(2,128)(2,1)S(1)} all-to-all(bf16[2,64,256]{2,0,1:T(2,128)(2,1)S(1)} %bitcast.23), channel_id=1, replica_groups=mesh['z'=8,'x'=4,'core'=2,'head'=8] {'z','x','core'}, dimensions={1} | all-to-all | bytes 131072 | tf_op jit(solution)/shard_map/all_to_all | solution.py:353
  95.1 0.6 copy.17
  (7 shorter events, 0.1 us)
Async XLA Ops:
  0.0 16.7 %copy-start.5 = (pred[128]{0:T(512)(128)(4,1)S(1)}, pred[128]{0:T(512)(128)(4,1)}, u32[]{:S(2)}) copy-start(pred[128]{0:T(512)(128)(4,1)} %constant.62.clone) | copy-start | bytes 388
  0.0 16.7 %copy-start.4 = (pred[128]{0:T(512)(128)(4,1)S(1)}, pred[128]{0:T(512)(128)(4,1)}, u32[]{:S(2)}) copy-start(pred[128]{0:T(512)(128)(4,1)} %constant.60.clone) | copy-start | bytes 388
  0.0 16.6 %copy-start.3 = (s32[4]{0:T(128)S(1)}, s32[4]{0:T(128)}, u32[]{:S(2)}) copy-start(s32[4]{0:T(128)} %param.20) | copy-start | bytes 52
  0.0 16.7 %copy-start.2 = (s32[4,256]{1,0:T(4,128)S(1)}, s32[4,256]{1,0:T(4,128)}, u32[]{:S(2)}) copy-start(s32[4,256]{1,0:T(4,128)} %param.19) | copy-start | bytes 12292
  11.9 14.1 %all-to-all-start = ((s16[8,96,128]{2,1,0:T(8,128)(2,1)}), s16[8,96,128]{2,1,0:T(8,128)(2,1)S(1)}, u32[]{:S(2)}, u32[]{:S(2)}) async-start(s16[8,96,128]{2,1,0:T(8,128)(2,1)} %bitcast.1), calls=%async_computation | async-start | bytes 393216 | tf_op jit(solution)/shard_map/all_to_all | solution.py:353
  26.3 38.2 %copy-start = (bf16[2048,256]{1,0:T(8,128)(2,1)S(1)}, bf16[2048,256]{1,0:T(8,128)(2,1)}, u32[]{:S(2)}) copy-start(bf16[2048,256]{1,0:T(8,128)(2,1)} %w_ref.1) | copy-start | bytes 3145732
  38.4 40.4 %copy-start.1 = (s32[4]{0:T(128)S(1)}, s32[4]{0:T(128)}, u32[]{:S(2)}) copy-start(s32[4]{0:T(128)} %owners_ref.1) | copy-start | bytes 52

commit v7 on v6

--- a/solution.py
+++ b/solution.py
@@ -357,7 +357,7 @@
     core = lax.axis_index("core").astype(jnp.int32).reshape(1)
 
     with jax.named_scope("project"):
-        chunks = 4
+        chunks = 2
         parts = call(
             project_kernel,
             jax.ShapeDtypeStruct((8 * (heads + 3), HD), F32),

time: 96.1 us -> 95.9 us (level)
  no operation moved by 1% of the time
where the time goes in v7:
time: 95.9 us; the launch traced here: 95.5 us
  blocking collectives  73.9 us (77%)
  waiting for transfers between devices  6.94 us (7%)
  Pallas kernels  6.79 us (7%)
  starting transfers between devices  4.66 us (5%)
  local copies, waits for them, and re-layouts  2.42 us (3%)
    all_to_all x5, blocking collectives, exchange(): return lax.all_to_all(x, axis, dim, dim, tiled=True)  62.7 us
    all_gather x2, blocking collectives, body(): parts = lax.all_gather(parts, 'core', axis=0, tiled=True)  11.2 us
    all_to_all x1, waiting for transfers between devices, exchange(): return lax.all_to_all(x, axis, dim, dim, tiled=True)  6.94 us
    all_to_all x1, starting transfers between devices, exchange(): return lax.all_to_all(x, axis, dim, dim, tiled=True)  4.66 us
    pallas_call x1, Pallas kernels, body(): call(project_kernel, jax.ShapeDtypeStruct((8 * (heads + 3), HD), F32), [h...  2.22 us
    pallas_call x1, Pallas kernels, body(): call(functools.partial(attend_kernel, HD ** (-0.5), 1.0 / width_total), j...  2.04 us
  transfers between devices with their start and end apart: 1, of which 1 were waited for; matrix products, arithmetic and copies ran while one was open for 3% of the time, Pallas kernels for 0%

profile of v7, /device:TPU:1, one launch (start us, length us, event | category | flops | bytes accessed | tf_op | source)
XLA Modules:
  0.0 95.5 jit_solution(10160545491963659666)
XLA Ops:
  0.0 0.0 copy-start.5
  0.0 0.0 copy-start.4
  0.0 0.0 copy-start.3
  0.0 0.0 copy-start.2
  0.0 2.2 %project.1 = f32[152,128]{1,0:T(8,128)} custom-call(bf16[2,4,256]{2,1,0:T(4,128)(2,1)} %hidden_hbm.1, bf16[256]{0:T(256)(128)(2,1)} %gain_hbm.1, bf16[256,2048]{1,0:T(8,128)(2,1)} %wq_hbm.1, bf16[256,256]{1,0:T(8,128)(2,1)} %wkv_hbm.1), custom_call_target="tpu_custom_call" | custom-call | tf_op jit(solution)/shard_map/project/pallas_call | solution.py:361
  2.3 8.7 %all_gather.6.rows_ref = f32[304,128]{1,0:T(8,128)S(1)} all-gather(f32[152,128]{1,0:T(8,128)} %project.1), channel_id=1, replica_groups=mesh['z'=8,'x'=4,'core'=2,'head'=8] {'core'}, dimensions={0}, use_global_device_ids=true | all-gather | bytes 233472 | tf_op jit(solution)/shard_map/all_gather | solution.py:374
  10.9 0.8 pair.1
  11.7 4.7 %all-to-all-start = ((s16[8,96,128]{2,1,0:T(8,128)(2,1)}), s16[8,96,128]{2,1,0:T(8,128)(2,1)S(1)}, u32[]{:S(2)}, u32[]{:S(2)}) async-start(s16[8,96,128]{2,1,0:T(8,128)(2,1)} %bitcast.1), calls=%async_computation | async-start | bytes 393216 | tf_op jit(solution)/shard_map/all_to_all | solution.py:353
  16.4 0.0 copy-done.3
  16.4 0.1 subtract_clamp_fusion
  16.5 0.0 copy-done.5
  16.5 0.0 copy-done.4
  16.5 0.0 copy-done.2
  16.5 0.3 select_reduce_fusion
  16.9 1.7 %fusion.1 = (bf16[4096,128]{1,0:T(8,128)(2,1)S(1)}, bf16[4096,128]{1,0:T(8,128)(2,1)S(1)}) fusion(bf16[4096,256]{1,0:T(8,128)(2,1)} %bitcast.24), kind=kLoop, calls=%fused_computation.15 | loop fusion | bytes 4194304 | tf_op jit(solution)/shard_map/slice | solution.py:401
  18.6 0.1 convert_element_type.14
  18.7 0.1 fusion
  18.8 0.1 pad_maximum_fusion
  18.9 6.9 %all-to-all-done = s16[8,96,128]{2,1,0:T(8,128)(2,1)S(1)} async-done(((s16[8,96,128]{2,1,0:T(8,128)(2,1)}), s16[8,96,128]{2,1,0:T(8,128)(2,1)S(1)}, u32[]{:S(2)}, u32[]{:S(2)}) %all-to-all-start) | async-done | bytes 196640 | tf_op jit(solution)/shard_map/all_to_all | solution.py:353
  25.8 0.2 sum.1
  26.1 0.0 copy-start
  26.1 12.1 %all_to_all.34 = s16[8,96,128]{2,1,0:T(8,128)(2,1)S(1)} all-to-all(s16[8,96,128]{2,1,0:T(8,128)(2,1)S(1)} %bitcast.16), channel_id=1, replica_groups=mesh['z'=8,'x'=4,'core'=2,'head'=8] {'x','core'}, dimensions={0} | all-to-all | bytes 393216 | tf_op jit(solution)/shard_map/all_to_all | solution.py:353
  38.2 0.0 copy-start.1
  38.2 2.0 %attend.1 = f32[136,128]{1,0:T(8,128)S(1)} custom-call(s16[768,128]{1,0:T(8,128)(2,1)S(1)} %bitcast.14, f32[8,128]{1,0:T(8,128)S(1)} %get-tuple-element.20.cos_ref, f32[8,128]{1,0:T(8,128)S(1)} %get-tuple-element.21.sin_ref, s32[8,128]{1,0:T(8,128)S(1)} %pad_add_fusion.limit_ref, bf16[4096,128]{1,0:T(8,128)(2,1)S(1)} %get-tuple-element.23.keys_ref, ...), custom_call_target="tpu_custom_call" | custom-call | tf_op jit(solution)/shard_map/attend/pallas_call | solution.py:414
  40.2 2.5 %all_gather.7.rows_ref = f32[272,128]{1,0:T(8,128)S(1)} all-gather(f32[136,128]{1,0:T(8,128)S(1)} %attend.1), channel_id=1, replica_groups=mesh['z'=8,'x'=4,'core'=2,'head'=8] {'core'}, dimensions={0}, use_global_device_ids=true | all-gather | bytes 208896 | tf_op jit(solution)/shard_map/all_gather | solution.py:420
  42.7 0.2 join.1
  42.9 11.6 %all_to_all.35 = bf16[8,80,128]{2,1,0:T(8,128)(2,1)S(1)} all-to-all(bf16[8,80,128]{2,1,0:T(8,128)(2,1)S(1)} %bitcast.18), channel_id=1, replica_groups=mesh['z'=8,'x'=4,'core'=2,'head'=8] {'z'}, dimensions={0} | all-to-all | bytes 327680 | tf_op jit(solution)/shard_map/all_to_all | solution.py:353
  54.5 0.3 merge.1
  54.8 9.5 %all_to_all.36 = bf16[8,80,128]{2,1,0:T(8,128)(2,1)S(1)} all-to-all(bf16[8,80,128]{2,1,0:T(8,128)(2,1)S(1)} %bitcast.20), channel_id=1, replica_groups=mesh['z'=8,'x'=4,'core'=2,'head'=8] {'x','core'}, dimensions={0} | all-to-all | bytes 327680 | tf_op jit(solution)/shard_map/all_to_all | solution.py:353
  64.3 0.0 copy-done
  64.3 0.5 output.1
  64.7 13.9 %all_to_all.37 = f32[8,8,256]{2,1,0:T(8,128)S(1)} all-to-all(f32[8,8,256]{2,1,0:T(8,128)S(1)} %bitcast.21), channel_id=1, replica_groups=mesh['z'=8,'x'=4,'core'=2,'head'=8] {'head'}, dimensions={0} | all-to-all | bytes 131072 | tf_op jit(solution)/shard_map/all_to_all | solution.py:353
  78.6 0.0 copy-done.1
  78.6 0.6 deliver.1
  79.2 15.7 %all_to_all.38 = bf16[2,64,256]{2,0,1:T(2,128)(2,1)S(1)} all-to-all(bf16[2,64,256]{2,0,1:T(2,128)(2,1)S(1)} %bitcast.23), channel_id=1, replica_groups=mesh['z'=8,'x'=4,'core'=2,'head'=8] {'z','x','core'}, dimensions={1} | all-to-all | bytes 131072 | tf_op jit(solution)/shard_map/all_to_all | solution.py:353
  94.9 0.6 copy.17
  (7 shorter events, 0.1 us)
Async XLA Ops:
  0.0 16.5 %copy-start.5 = (pred[128]{0:T(512)(128)(4,1)S(1)}, pred[128]{0:T(512)(128)(4,1)}, u32[]{:S(2)}) copy-start(pred[128]{0:T(512)(128)(4,1)} %constant.62.clone) | copy-start | bytes 388
  0.0 16.5 %copy-start.4 = (pred[128]{0:T(512)(128)(4,1)S(1)}, pred[128]{0:T(512)(128)(4,1)}, u32[]{:S(2)}) copy-start(pred[128]{0:T(512)(128)(4,1)} %constant.60.clone) | copy-start | bytes 388
  0.0 16.4 %copy-start.3 = (s32[4]{0:T(128)S(1)}, s32[4]{0:T(128)}, u32[]{:S(2)}) copy-start(s32[4]{0:T(128)} %param.20) | copy-start | bytes 52
  0.0 16.5 %copy-start.2 = (s32[4,256]{1,0:T(4,128)S(1)}, s32[4,256]{1,0:T(4,128)}, u32[]{:S(2)}) copy-start(s32[4,256]{1,0:T(4,128)} %param.19) | copy-start | bytes 12292
  11.7 14.1 %all-to-all-start = ((s16[8,96,128]{2,1,0:T(8,128)(2,1)}), s16[8,96,128]{2,1,0:T(8,128)(2,1)S(1)}, u32[]{:S(2)}, u32[]{:S(2)}) async-start(s16[8,96,128]{2,1,0:T(8,128)(2,1)} %bitcast.1), calls=%async_computation | async-start | bytes 393216 | tf_op jit(solution)/shard_map/all_to_all | solution.py:353
  26.1 38.2 %copy-start = (bf16[2048,256]{1,0:T(8,128)(2,1)S(1)}, bf16[2048,256]{1,0:T(8,128)(2,1)}, u32[]{:S(2)}) copy-start(bf16[2048,256]{1,0:T(8,128)(2,1)} %w_ref.1) | copy-start | bytes 3145732
  38.2 40.4 %copy-start.1 = (s32[4]{0:T(128)S(1)}, s32[4]{0:T(128)}, u32[]{:S(2)}) copy-start(s32[4]{0:T(128)} %owners_ref.1) | copy-start | bytes 52
